TPU v7x, 32 devices: a whole 2x2x4 slice. The times are simulated.
32 devices in a mesh: dp: 8 (over y, x, core), mp: 4 (over z).
Axes of the slice: x: 2, y: 2, z: 4, core: 2. Of those that a mesh axis runs over, the one named last changes fastest.
Arguments:
- tokens: bfloat16 [8192, 2048], P('dp'), may hold values from -6 to 6
- lengths: int32 [8, 8], P('dp'), may hold values from 1 to 768, 1024 in all within a row
- attn_gain: float32 [2048], replicated, may hold values from 0.1 to 1.9
- attn_shift: float32 [2048], replicated, may hold values from -4 to 4
- mlp_gain: float32 [2048], replicated, may hold values from 0.1 to 1.9
- mlp_shift: float32 [2048], replicated, may hold values from -4 to 4
- qkv_weight: bfloat16 [2048, 6144], P(None, 'mp'), may hold values from -0.125 to 0.125
- qkv_bias: float32 [6144], P('mp'), may hold values from -4 to 4
- dense_weight: bfloat16 [2048, 2048], P('mp'), may hold values from -0.5 to 0.5
- up_weight: bfloat16 [2048, 8192], P(None, 'mp'), may hold values from -0.125 to 0.125
- up_bias: float32 [8192], P('mp'), may hold values from -6 to 6
- down_weight: bfloat16 [8192, 2048], P('mp'), may hold values from -0.0625 to 0.0625
- out_bias: float32 [2048], replicated, may hold values from -6 to 6
- cotangent: bfloat16 [8192, 2048], P('dp'), may hold values from -6 to 6
Outputs:
- layer_output: bfloat16 [8192, 2048], P('dp')
- input_grad: bfloat16 [8192, 2048], P('dp')
- attn_gain_grad: float32 [2048], P('dp')
- attn_shift_grad: float32 [2048], P('dp')
- mlp_gain_grad: float32 [2048], P('dp')
- mlp_shift_grad: float32 [2048], P('dp')
- qkv_weight_grad: float32 [2048, 6144], P('dp', 'mp')
- qkv_bias_grad: float32 [6144], P(('mp', 'dp'))
- dense_weight_grad: float32 [2048, 2048], P('mp', 'dp')
- up_weight_grad: float32 [2048, 8192], P('dp', 'mp')
- up_bias_grad: float32 [8192], P(('mp', 'dp'))
- down_weight_grad: float32 [8192, 2048], P('mp', 'dp')
- out_bias_grad: float32 [2048], P('dp')
Inputs may be any that keep to these rules, and one draw needn't show every extreme that they name: Each row holds 8 sequence lengths that add up to 1024; in every row the longest is exactly 768.
All inputs are finite; a program needn't handle non-finite values.
Results may differ from a plain program's by a relative error of at most 0.0095.
Values sent between devices are 32-bit elements; how exact they have to be, the bound alone decides.
A program may use at most 256 MiB of HBM per device.

v0:
```python
import math

import jax
import jax.numpy as jnp
from jax import lax
from jax.sharding import PartitionSpec as P

HEAD_DIM = 256
ROT = 64


EPSILON = 1e-05


def layer_norm(matrix, gain, shift):
    centred = matrix - jnp.mean(matrix, axis=-1, keepdims=True)
    spread = jnp.mean(centred * centred, axis=-1, keepdims=True)
    return centred * lax.rsqrt(spread + EPSILON) * gain + shift


def rotate(field, position):
    half = ROT // 2
    steps = jnp.arange(half, dtype=jnp.float32)
    freqs = jnp.exp(steps * (-2.0 * math.log(10000.0) / ROT))
    angle = position.astype(jnp.float32)[:, None] * freqs[None, :]
    cosine = jnp.concatenate([jnp.cos(angle), jnp.cos(angle)], axis=-1)[:, None, :]
    sine = jnp.concatenate([jnp.sin(angle), jnp.sin(angle)], axis=-1)[:, None, :]
    turned = field[..., :ROT]
    swapped = jnp.concatenate([-turned[..., half:], turned[..., :half]], axis=-1)
    return jnp.concatenate([turned * cosine + swapped * sine, field[..., ROT:]], axis=-1)


def layout(lengths_row, count):
    ends = jnp.cumsum(lengths_row)
    places = jnp.arange(count, dtype=jnp.int32)
    passed = (places[:, None] >= ends[None, :]).astype(jnp.int32)
    segment = jnp.sum(passed, axis=1)
    position = places - jnp.sum(passed * lengths_row[None, :], axis=1)
    return (segment, position)


def contract_rows(left, right):
    return lax.dot_general(
        left, right, (((0,), (0,)), ((), ())), preferred_element_type=jnp.float32
    )


def contract_cols(left, right):
    return lax.dot_general(
        left, right, (((1,), (1,)), ((), ())), preferred_element_type=jnp.float32
    )


def per_device(
    tokens,
    lengths,
    attn_gain,
    attn_shift,
    mlp_gain,
    mlp_shift,
    qkv_weight,
    qkv_bias,
    dense_weight,
    up_weight,
    up_bias,
    down_weight,
    out_bias,
    cotangent,
):
    count = tokens.shape[0]
    local_heads = qkv_weight.shape[1] // (3 * HEAD_DIM)
    width = local_heads * HEAD_DIM
    segment, position = layout(lengths[0], count)
    block = min(512, count)
    blocks = count // block
    scale = 1.0 / math.sqrt(HEAD_DIM)
    places = jnp.arange(count, dtype=jnp.int32)
    inputs = tokens.astype(jnp.float32)
    normed_attn, attn_back = jax.vjp(layer_norm, inputs, attn_gain, attn_shift)
    normed_mlp, mlp_back = jax.vjp(layer_norm, inputs, mlp_gain, mlp_shift)
    attn_entry = normed_attn.astype(jnp.bfloat16)
    mlp_entry = normed_mlp.astype(jnp.bfloat16)
    joined = jnp.dot(attn_entry, qkv_weight, preferred_element_type=jnp.float32) + qkv_bias
    joined = joined.reshape(count, local_heads, 3, HEAD_DIM)
    turned_query, query_back = jax.vjp(lambda field: rotate(field, position), joined[:, :, 0])
    turned_key, key_back = jax.vjp(lambda field: rotate(field, position), joined[:, :, 1])
    queries = turned_query.astype(jnp.bfloat16)
    keys_low = turned_key.astype(jnp.bfloat16)
    values_low = joined[:, :, 2].astype(jnp.bfloat16)

    def masked_scores(start):
        query_block = lax.dynamic_slice_in_dim(queries, start, block, 0)
        scores = (
            jnp.einsum("bhd,shd->hbs", query_block, keys_low, preferred_element_type=jnp.float32)
            * scale
        )
        rows_here = start + jnp.arange(block, dtype=jnp.int32)
        segment_block = lax.dynamic_slice_in_dim(segment, start, block, 0)
        allowed = (segment_block[:, None] == segment[None, :]) & (
            rows_here[:, None] >= places[None, :]
        )
        return (jnp.where(allowed[None], scores, -1e30), query_block)

    def forward_block(index):
        scores, query_block = masked_scores(index * block)
        peak = jnp.max(scores, axis=-1, keepdims=True)
        expo = jnp.exp(scores - peak)
        total = jnp.sum(expo, axis=-1, keepdims=True)
        probs = expo / total
        result = jnp.einsum(
            "hbs,shd->bhd",
            probs.astype(jnp.bfloat16),
            values_low,
            preferred_element_type=jnp.float32,
        )
        return (result, peak[..., 0] + jnp.log(total[..., 0]))

    attended, log_total = lax.map(forward_block, jnp.arange(blocks, dtype=jnp.int32))
    attended_low = attended.reshape(count, width).astype(jnp.bfloat16)
    hidden_pre = jnp.dot(mlp_entry, up_weight, preferred_element_type=jnp.float32) + up_bias
    activated, gelu_back = jax.vjp(lambda field: jax.nn.gelu(field, approximate=False), hidden_pre)
    hidden_low = activated.astype(jnp.bfloat16)
    partial_sum = jnp.dot(attended_low, dense_weight, preferred_element_type=jnp.float32) + jnp.dot(
        hidden_low, down_weight, preferred_element_type=jnp.float32
    )
    branch = lax.psum(partial_sum, "mp")
    layer_output = (inputs + branch + out_bias).astype(jnp.bfloat16)
    out_bias_grad = jnp.sum(cotangent.astype(jnp.float32), axis=0)
    dense_grad = contract_rows(attended_low, cotangent)
    down_grad = contract_rows(hidden_low, cotangent)
    hidden_grad = gelu_back(contract_cols(cotangent, down_weight))[0].astype(jnp.bfloat16)
    up_grad = contract_rows(mlp_entry, hidden_grad)
    up_bias_grad = jnp.sum(hidden_grad.astype(jnp.float32), axis=0)
    mlp_entry_grad = contract_cols(hidden_grad, up_weight)
    attended_grad = (
        contract_cols(cotangent, dense_weight)
        .reshape(count, local_heads, HEAD_DIM)
        .astype(jnp.bfloat16)
    )

    def backward_block(carry, index):
        key_total, value_total = carry
        start = index * block
        scores, query_block = masked_scores(start)
        probs = jnp.exp(scores - log_total[index][:, :, None])
        grad_block = lax.dynamic_slice_in_dim(attended_grad, start, block, 0)
        prob_grad = jnp.einsum(
            "bhd,shd->hbs", grad_block, values_low, preferred_element_type=jnp.float32
        )
        inner = jnp.sum(probs * prob_grad, axis=-1, keepdims=True)
        score_grad = (probs * (prob_grad - inner)).astype(jnp.bfloat16)
        query_part = (
            jnp.einsum("hbs,shd->bhd", score_grad, keys_low, preferred_element_type=jnp.float32)
            * scale
        )
        key_total = (
            key_total
            + jnp.einsum(
                "hbs,bhd->shd", score_grad, query_block, preferred_element_type=jnp.float32
            )
            * scale
        )
        value_total = value_total + jnp.einsum(
            "hbs,bhd->shd",
            probs.astype(jnp.bfloat16),
            grad_block,
            preferred_element_type=jnp.float32,
        )
        return ((key_total, value_total), query_part)

    empty = jnp.zeros((count, local_heads, HEAD_DIM), jnp.float32)
    (key_grad, value_grad), query_grad = lax.scan(
        backward_block, (empty, empty), jnp.arange(blocks, dtype=jnp.int32)
    )
    query_grad = query_grad.reshape(count, local_heads, HEAD_DIM)
    joined_grad = jnp.stack([query_back(query_grad)[0], key_back(key_grad)[0], value_grad], axis=2)
    joined_grad = joined_grad.reshape(count, 3 * width).astype(jnp.bfloat16)
    qkv_grad = contract_rows(attn_entry, joined_grad)
    qkv_bias_grad = jnp.sum(joined_grad.astype(jnp.float32), axis=0)
    attn_entry_grad = contract_cols(joined_grad, qkv_weight)
    attn_summed, mlp_summed = lax.psum((attn_entry_grad, mlp_entry_grad), "mp")
    attn_parts = attn_back(attn_summed)
    mlp_parts = mlp_back(mlp_summed)
    input_grad = cotangent.astype(jnp.float32) + attn_parts[0] + mlp_parts[0]
    norm_grads = (attn_parts[1], attn_parts[2], mlp_parts[1], mlp_parts[2])
    every_sum = (
        lax.psum_scatter(qkv_grad, "dp", scatter_dimension=0, tiled=True),
        lax.psum_scatter(qkv_bias_grad, "dp", scatter_dimension=0, tiled=True),
        lax.psum_scatter(dense_grad, "dp", scatter_dimension=1, tiled=True),
        lax.psum_scatter(up_grad, "dp", scatter_dimension=0, tiled=True),
        lax.psum_scatter(up_bias_grad, "dp", scatter_dimension=0, tiled=True),
        lax.psum_scatter(down_grad, "dp", scatter_dimension=1, tiled=True),
        lax.psum_scatter(out_bias_grad, "dp", scatter_dimension=0, tiled=True),
        lax.psum_scatter(norm_grads[0], "dp", scatter_dimension=0, tiled=True),
        lax.psum_scatter(norm_grads[1], "dp", scatter_dimension=0, tiled=True),
        lax.psum_scatter(norm_grads[2], "dp", scatter_dimension=0, tiled=True),
        lax.psum_scatter(norm_grads[3], "dp", scatter_dimension=0, tiled=True),
    )
    (
        qkv_total,
        qkv_bias_total,
        dense_total,
        up_total,
        up_bias_total,
        down_total,
        out_bias_total,
        gain_first,
        shift_first,
        gain_second,
        shift_second,
    ) = every_sum
    return (
        layer_output,
        input_grad.astype(jnp.bfloat16),
        gain_first,
        shift_first,
        gain_second,
        shift_second,
        qkv_total,
        qkv_bias_total,
        dense_total,
        up_total,
        up_bias_total,
        down_total,
        out_bias_total,
    )


def solution(mesh):
    in_specs = (
        P("dp", None),
        P("dp", None),
        P(),
        P(),
        P(),
        P(),
        P(None, "mp"),
        P("mp"),
        P("mp", None),
        P(None, "mp"),
        P("mp"),
        P("mp", None),
        P(),
        P("dp", None),
    )
    out_specs = (
        P("dp", None),
        P("dp", None),
        P("dp"),
        P("dp"),
        P("dp"),
        P("dp"),
        P("dp", "mp"),
        P(("mp", "dp")),
        P("mp", "dp"),
        P("dp", "mp"),
        P(("mp", "dp")),
        P("mp", "dp"),
        P("dp"),
    )
    return jax.shard_map(
        per_device, mesh=mesh, in_specs=in_specs, out_specs=out_specs, check_vma=False
    )
```

profile of v0, /device:TPU:0, one launch (start us, length us, event | category | flops | bytes accessed | tf_op | source)
XLA Modules:
  0.0 1133.9 jit_solution(4099500284698491343)
XLA Ops:
  14.7 11.7 %convolution_add_fusion = f32[1024,1536]{1,0:T(8,128)} fusion(bf16[2048,1536]{1,0:T(8,128)(2,1)} %param.24, f32[1536]{0:T(1024)S(1)} %copy-done.43, bf16[1024,2048]{1,0:T(8,128)(2,1)S(1)} %copy-done.1, f32[2048]{0:T(1024)S(1)} %copy-done.44, f32[2048]{0:T(1024)S(1)} %copy-done.31, f32[1024]{0:T(1024)S(1)} %fusion.73, f32[1024]{0:T(1024)S(1)} %broadcast_multiply_fusion.1), kind=kOutput, calls=%fused_computation.99 | convolution fusion | flops 6456606720 | bytes 16807936 | tf_op jit(solution)/shard_map/dot_general | solution.py:83
  26.4 6.6 copy.72
  56.2 16.0 %while.28 = (s32[]{:T(128)}, bf16[2,512,2,256]{3,1,2,0:T(8,128)(2,1)}, f32[2,2,512]{2,1,0:T(2,128)S(1)}, s32[2]{0:T(128)S(1)}, s32[1024]{0:T(1024)S(1)}, /*index...) while((s32[]{:T(128)}, ...), condition=%wide.region_8.9_spmd.clone, body=%wide.region_5.0_spmd.clone.sunk | while | flops 1087897088 | bytes 26786052 | solution.py:118
  72.2 5.5 convolution_convert_fusion
  77.8 35.3 %while.29 = (s32[]{:T(128)}, f32[1024,2,256]{0,2,1:T(8,128)}, f32[1024,2,256]{0,2,1:T(8,128)}, f32[2,512,2,256]{3,1,0,2:T(8,128)}, s32[2]{0:T(128)S(1)}, /*index...) while((s32[]{:T(128)}, f32[1024,2,256]{0,2,1:T(8,128)}, ...), condition=%wide.region_12.13_spmd.clone, body=%wide.region_10.12_spmd.clone.sunk | while | flops 2704539136 | bytes 94415344 | solution.py:172
  84.0 4.0 bitcast_add_fusion.5
  101.2 4.7 bitcast_add_fusion.5
  115.4 3.5 split.32
  134.6 9.4 fusion.89
  144.1 11.6 %fusion.76 = f32[1024,2048]{1,0:T(8,128)S(1)} fusion(bf16[2048,2048]{1,0:T(8,128)(2,1)} %param.27, bf16[1024,2048]{1,0:T(8,128)(2,1)S(1)} %copy-done.2, f32[2048]{0:T(1024)S(1)} %copy-done.46, f32[2048]{0:T(1024)S(1)} %copy-done.29, f32[1024]{0:T(1024)S(1)} %copy-done.36, f32[1024]{0:T(1024)S(1)} %copy-done.27), kind=kOutput, calls=%fused_computation.146 | convolution fusion | flops 8602517504 | bytes 20996096 | tf_op jit(solution)/shard_map/dot_general | solution.py:120
  155.8 30.0 %convert_reduce_fusion.2 = (f32[2048]{0:T(1024)}, bf16[1024,2048]{1,0:T(8,128)(2,1)}, f32[1024,2048]{1,0:T(8,128)}) fusion(f32[1024,2048]{1,0:T(8,128)S(1)} %fusion.76, f32[2048]{0:T(1024)S(1)} %copy-done.39, bf16[1024,2048]{1,0:T(8,128)(2,1)S(1)} %copy-done.10, bf16[2048,2048]{1,0:T(8,128)(2,1)S(1)} %bitcast.120), kind=kOutput, calls=%fused_computation.81 | convolution fusion | flops 8747218944 | bytes 33570816 | tf_op jit(solution)/shard_map/dot_general | solution.py:49
  185.8 8.0 multiply_convert_fusion.1
  193.8 12.8 %fusion.88 = f32[1024,2048]{1,0:T(8,128)S(1)} fusion(bf16[1024,2048]{1,0:T(8,128)(2,1)S(1)} %multiply_convert_fusion.1, bf16[2048,2048]{1,0:T(8,128)(2,1)} %param.29), kind=kOutput, calls=%fused_computation.154 | convolution fusion | flops 8589934592 | bytes 20971520 | tf_op jit(solution)/shard_map/dot_general | solution.py:123
  206.6 13.3 %fusion.90 = f32[1024,2048]{1,0:T(8,128)} fusion(bf16[1024,2048]{1,0:T(8,128)(2,1)S(1)} %copy-done.49, bf16[2048,2048]{1,0:T(8,128)(2,1)} %param.27), kind=kOutput, calls=%fused_computation.156 | convolution fusion | flops 8589934592 | bytes 20971520 | tf_op jit(solution)/shard_map/dot_general | solution.py:49
  220.0 5.6 convolution_add_fusion.1
  225.9 6.5 fusion.91
  232.6 15.7 %fusion.78 = f32[2048,1536]{1,0:T(8,128)} fusion(bf16[1024,1536]{0,1:T(8,128)(2,1)} %bitcast.114, bf16[1024,2048]{1,0:T(8,128)(2,1)} %param.18, f32[2048]{0:T(1024)S(1)} %copy-done.45, f32[2048]{0:T(1024)S(1)} %copy-done.32, f32[1024]{0:T(1024)S(1)} %copy-done.37, f32[1024]{0:T(1024)S(1)} %copy-done.28), kind=kOutput, calls=%fused_computation.147 | convolution fusion | flops 6455033856 | bytes 19947520 | tf_op jit(solution)/shard_map/dot_general | solution.py:43
  249.0 15.7 %fusion.74 = f32[2048,2048]{1,0:T(8,128)} fusion(bf16[1024,2048]{1,0:T(8,128)(2,1)} %get-tuple-element.323, bf16[1024,2048]{1,0:T(8,128)(2,1)} %param.18, f32[2048]{0:T(1024)S(1)} %copy-done.47, f32[2048]{0:T(1024)S(1)} %copy-done.30, f32[1024]{0:T(1024)S(1)} %copy-done.37, f32[1024]{0:T(1024)S(1)} %copy-done.28), kind=kOutput, calls=%fused_computation.145 | convolution fusion | flops 8602517504 | bytes 25190400 | tf_op jit(solution)/shard_map/dot_general | solution.py:43
  265.1 15.3 %fusion.92 = f32[2048,2048]{1,0:T(8,128)} fusion(bf16[1024,2048]{1,0:T(8,128)(2,1)} %copy-done.19, bf16[1024,2048]{1,0:T(8,128)(2,1)} %param.31), kind=kOutput, calls=%fused_computation.158 | convolution fusion | flops 8589934592 | bytes 25165824 | tf_op jit(solution)/shard_map/dot_general | solution.py:43
  283.0 781.0 %all-reduce.19.cloned.1.call-done = (f32[1024,2048]{1,0:T(8,128)}, f32[1024,2048]{1,0:T(8,128)}, f32[1024,2048]{1,0:T(8,128)}) async-done(((f32[1024,2048]{1,0:T(8,128)}, f32[1024,2048]{1,0:T(8,128)}, f32[1024,2048]{1,0:T(8,128)}), (f32[1024,2048]{1,0:T(8,128)}, f32[1024,2048]{1,0:T(8,128)}, f32[1024,2048]{1,0:T(8,128)})) %all-reduce.19.cloned.1.call-update) | async-done | bytes 25165840 | tf_op jit(solution)/shard_map/psum | solution.py:126
  1063.9 8.9 fusion.84
  1077.0 7.2 fusion.56
  1084.2 12.7 %convert_reduce_fusion.1 = (f32[2048]{0:T(1024)S(1)}, bf16[1024,2048]{1,0:T(8,128)(2,1)}, bf16[1024,2048]{1,0:T(8,128)(2,1)}) fusion(bf16[1024,2048]{1,0:T(8,128)(2,1)} %param.31, f32[1024]{0:T(1024)S(1)} %negate_multiply_fusion.1, f32[1024]{0:T(1024)S(1)} %get-tuple-element.355, f32[1024,2048]{1,0:T(8,128)S(1)} %copy-done.6, f32[2048]{0:T(1024)S(1)} %copy-done.30, ...), kind=kLoop, calls=%fused_computation.65 | loop fusion | flops 46135296 | bytes 42000384 | tf_op jit(solution)/shard_map/reduce_sum | solution.py:128
  1096.9 24.6 %all-reduce.15 = (f32[2048]{0:T(1024)S(1)}, f32[2048]{0:T(1024)S(1)}, f32[2048]{0:T(1024)S(1)}, f32[2048]{0:T(1024)S(1)}, f32[1536]{0:T(1024)S(1)}, /*index=5*/f32[2048]{0:T(1024)S(1)}, f32[2048]{0:T(1024)S(1)}) all-reduce(f32[2048]{0:T(1024)S(1)} %get-tuple-element.271, ...), channel_id=2, replica_groups=mesh['dp'=8,'mp'=4] {'dp'}, use_global_device_ids=true, to_apply=%region_20.21.clone | all-reduce | flops 13824 | bytes 110592
  (233 shorter events, 94.5 us)
Async XLA Ops:
  8.0 64.2 %copy-start = (bf16[512,2048]{1,0:T(8,128)(2,1)S(1)}, bf16[512,2048]{1,0:T(8,128)(2,1)}, u32[]{:S(2)}) copy-start(bf16[512,2048]{1,0:T(8,128)(2,1)} %param.26) | copy-start | bytes 6291460
  8.1 1055.9 %all-reduce.19.cloned.1.call-start = ((), (), s32[]{:S(2)}) async-start(), calls=%async_computation.8 | async-start | bytes 50331648 | tf_op jit(solution)/shard_map/psum | solution.py:126
  14.6 11.8 %copy-start.33 = (f32[1024]{0:T(1024)}, f32[1024]{0:T(1024)S(1)}, u32[]{:S(2)}) copy-start(f32[1024]{0:T(1024)S(1)} %fusion.57) | copy-start | bytes 12292
  14.7 11.7 %copy-start.35 = (f32[1024]{0:T(1024)}, f32[1024]{0:T(1024)S(1)}, u32[]{:S(2)}) copy-start(f32[1024]{0:T(1024)S(1)} %fusion.73) | copy-start | bytes 12292
  118.9 10.9 copy-start.22
  134.5 9.5 copy-start.2
  134.5 9.5 copy-start.27
  134.5 9.5 copy-start.29
  134.6 9.5 copy-start.36
  134.6 21.1 %slice-start = ((s8[8388608]{0:T(1024)(128)(4,1)}), s8[4194304]{0:T(1024)(128)(4,1)S(1)}, s32[]{:S(2)}) async-start(s8[8388608]{0:T(1024)(128)(4,1)} %bitcast.119), calls=%async_computation.9 | async-start | bytes 8388608
  144.0 11.7 %copy-start.10 = (bf16[1024,2048]{1,0:T(8,128)(2,1)S(1)}, bf16[1024,2048]{1,0:T(8,128)(2,1)}, u32[]{:S(2)}) copy-start(bf16[1024,2048]{1,0:T(8,128)(2,1)} %param.31) | copy-start | bytes 12582916
  144.1 11.7 %copy-start.39 = (f32[2048]{0:T(1024)S(1)}, f32[2048]{0:T(1024)}, u32[]{:S(2)}) copy-start(f32[2048]{0:T(1024)} %param.28) | copy-start | bytes 24580
  144.1 11.7 %slice-start.1 = ((s8[8388608]{0:T(1024)(128)(4,1)}), s8[4194304]{0:T(1024)(128)(4,1)S(1)}, s32[]{:S(2)}) async-start(s8[8388608]{0:T(1024)(128)(4,1)} %bitcast.119), calls=%async_computation.10 | async-start | bytes 8388608
  155.8 30.0 %copy-start.12 = (f32[1024,2048]{1,0:T(8,128)}, f32[1024,2048]{1,0:T(8,128)S(1)}, u32[]{:S(2)}) copy-start(f32[1024,2048]{1,0:T(8,128)S(1)} %fusion.76) | copy-start | bytes 25165828
  193.8 12.8 %copy-start.19 = (bf16[1024,2048]{1,0:T(8,128)(2,1)}, bf16[1024,2048]{1,0:T(8,128)(2,1)S(1)}, u32[]{:S(2)}) copy-start(bf16[1024,2048]{1,0:T(8,128)(2,1)S(1)} %multiply_convert_fusion.1) | copy-start | bytes 12582916
  193.8 12.8 %copy-start.49 = (bf16[1024,2048]{1,0:T(8,128)(2,1)S(1)}, bf16[1024,2048]{1,0:T(8,128)(2,1)}, u32[]{:S(2)}) copy-start(bf16[1024,2048]{1,0:T(8,128)(2,1)} %get-tuple-element.323) | copy-start | bytes 12582916
  206.6 13.3 %copy-start.11 = (bf16[128,8,2,256]{3,1,2,0:T(8,128)(2,1)S(1)}, bf16[128,8,2,256]{3,1,2,0:T(8,128)(2,1)}, u32[]{:S(2)}) copy-start(bf16[128,8,2,256]{3,1,2,0:T(8,128)(2,1)} %copy.116) | copy-start | bytes 3145732
  225.7 900.2 %reduce-scatter.7.cloned.1.call-start = ((), (), s32[]{:S(2)}) async-start(), calls=%async_computation.5 | async-start | bytes 4718592 | tf_op jit(solution)/shard_map/reduce_scatter | solution.py:189
  232.5 893.4 %reduce-scatter.5.cloned.1.call-start = ((), (), s32[]{:S(2)}) async-start(), calls=%async_computation.4 | async-start | bytes 14155776 | tf_op jit(solution)/shard_map/reduce_scatter | solution.py:187
  248.4 877.5 %reduce-scatter.9.cloned.1.call-start = ((), (), s32[]{:S(2)}) async-start(), calls=%async_computation.6 | async-start | bytes 18874368 | tf_op jit(solution)/shard_map/reduce_scatter | solution.py:190
  264.8 861.1 %reduce-scatter.11.cloned.1.call-start = ((), (), s32[]{:S(2)}) async-start(), calls=%async_computation.7 | async-start | bytes 18874368 | tf_op jit(solution)/shard_map/reduce_scatter | solution.py:192
  1063.9 10.7 copy-start.6
  1063.9 13.1 %copy-start.7 = (f32[1024,2048]{1,0:T(8,128)S(1)}, f32[1024,2048]{1,0:T(8,128)}, u32[]{:S(2)}) copy-start(f32[1024,2048]{1,0:T(8,128)} %get-tuple-element.321) | copy-start | bytes 25165828
  1084.2 12.7 %copy-start.41 = (f32[2048]{0:T(1024)S(1)}, f32[2048]{0:T(1024)}, u32[]{:S(2)}) copy-start(f32[2048]{0:T(1024)} %get-tuple-element.322) | copy-start | bytes 24580
  (44 other events, 185.7 us)
Sparse Core Ops, SparseCore 0:
  225.7 838.1 all-reduce.18
Sparse Core Ops, SparseCore 1:
  232.6 53.8 reduce-scatter.6
  290.4 92.2 reduce-scatter.4
  386.7 115.8 reduce-scatter.8
  506.7 115.8 reduce-scatter.10
where the time goes:
time: 1140 us; the launch traced here: 1130 us
  waiting for transfers between devices  781 us (69%)
  matrix products  182 us (16%)
  other arithmetic  63.1 us (6%)
  local copies, waits for them, and re-layouts  57.4 us (5%)
  blocking collectives  24.6 us (2%)
  between operations  18.2 us (2%)
    psum x1, waiting for transfers between devices, per_device(): branch = lax.psum(partial_sum, 'mp')  781 us
    dot_general x4, matrix products, contract_cols(): lax.dot_general(left, right, (((1,), (1,)), ((), ())), preferred_element_...  58.3 us
    dot_general x4, matrix products, contract_rows(): lax.dot_general(left, right, (((0,), (0,)), ((), ())), preferred_element_...  53.3 us
    unnamed x1, blocking collectives  24.6 us
    unnamed x104, local copies, waits for them, and re-layouts  24.5 us
  transfers between devices with their start and end apart: 5, of which 1 were waited for; matrix products, arithmetic and copies ran while one was open for 8% of the time, Pallas kernels for 0%

commit v1 on v0

--- a/solution.py
+++ b/solution.py
@@ -1,3 +1,4 @@
+import functools
 import math
 
 import jax
@@ -10,12 +11,6 @@
 
 
 EPSILON = 1e-05
-
-
-def layer_norm(matrix, gain, shift):
-    centred = matrix - jnp.mean(matrix, axis=-1, keepdims=True)
-    spread = jnp.mean(centred * centred, axis=-1, keepdims=True)
-    return centred * lax.rsqrt(spread + EPSILON) * gain + shift
 
 
 def rotate(field, position):
@@ -51,7 +46,30 @@
     )
 
 
+def line_sum(part, size):
+    if size == 1:
+        return part
+    if size % 2:
+        return lax.psum(part, "mp")
+    index = lax.axis_index("mp")
+    half = size // 2
+    total = part
+    for hop in range(half - 1):
+        pairs = [(hop, hop + 1), (size - 1 - hop, size - 2 - hop)]
+        total = total + lax.ppermute(total, "mp", pairs)
+    total = total + lax.ppermute(total, "mp", [(half - 1, half), (half, half - 1)])
+    for hop in reversed(range(half - 1)):
+        pairs = [(hop + 1, hop), (size - 2 - hop, size - 1 - hop)]
+        came = lax.ppermute(total, "mp", pairs)
+        total = jnp.where((index == hop) | (index == size - 1 - hop), came, total)
+    return total
+
+
+CHUNK = 128
+
+
 def per_device(
+    mp_size,
     tokens,
     lengths,
     attn_gain,
@@ -76,10 +94,11 @@
     scale = 1.0 / math.sqrt(HEAD_DIM)
     places = jnp.arange(count, dtype=jnp.int32)
     inputs = tokens.astype(jnp.float32)
-    normed_attn, attn_back = jax.vjp(layer_norm, inputs, attn_gain, attn_shift)
-    normed_mlp, mlp_back = jax.vjp(layer_norm, inputs, mlp_gain, mlp_shift)
-    attn_entry = normed_attn.astype(jnp.bfloat16)
-    mlp_entry = normed_mlp.astype(jnp.bfloat16)
+    centred = inputs - jnp.mean(inputs, axis=-1, keepdims=True)
+    factor = lax.rsqrt(jnp.mean(centred * centred, axis=-1, keepdims=True) + EPSILON)
+    xhat = centred * factor
+    attn_entry = (xhat * attn_gain + attn_shift).astype(jnp.bfloat16)
+    mlp_entry = (xhat * mlp_gain + mlp_shift).astype(jnp.bfloat16)
     joined = jnp.dot(attn_entry, qkv_weight, preferred_element_type=jnp.float32) + qkv_bias
     joined = joined.reshape(count, local_heads, 3, HEAD_DIM)
     turned_query, query_back = jax.vjp(lambda field: rotate(field, position), joined[:, :, 0])
@@ -117,14 +136,25 @@
 
     attended, log_total = lax.map(forward_block, jnp.arange(blocks, dtype=jnp.int32))
     attended_low = attended.reshape(count, width).astype(jnp.bfloat16)
-    hidden_pre = jnp.dot(mlp_entry, up_weight, preferred_element_type=jnp.float32) + up_bias
-    activated, gelu_back = jax.vjp(lambda field: jax.nn.gelu(field, approximate=False), hidden_pre)
-    hidden_low = activated.astype(jnp.bfloat16)
-    partial_sum = jnp.dot(attended_low, dense_weight, preferred_element_type=jnp.float32) + jnp.dot(
-        hidden_low, down_weight, preferred_element_type=jnp.float32
-    )
-    branch = lax.psum(partial_sum, "mp")
-    layer_output = (inputs + branch + out_bias).astype(jnp.bfloat16)
+
+    chunk = min(CHUNK, count)
+    outputs, pres, hiddens = [], [], []
+    for first in range(0, count, chunk):
+        rows = slice(first, first + chunk)
+        pre = jnp.dot(mlp_entry[rows], up_weight, preferred_element_type=jnp.float32) + up_bias
+        hidden = jax.nn.gelu(pre, approximate=False).astype(jnp.bfloat16)
+        part = jnp.dot(
+            attended_low[rows], dense_weight, preferred_element_type=jnp.float32
+        ) + jnp.dot(hidden, down_weight, preferred_element_type=jnp.float32)
+        branch = line_sum(part, mp_size)
+        outputs.append((inputs[rows] + branch + out_bias).astype(jnp.bfloat16))
+        pres.append(pre)
+        hiddens.append(hidden)
+    layer_output = jnp.concatenate(outputs)
+    hidden_pre = jnp.concatenate(pres)
+    hidden_low = jnp.concatenate(hiddens)
+    _, gelu_back = jax.vjp(lambda field: jax.nn.gelu(field, approximate=False), hidden_pre)
+
     out_bias_grad = jnp.sum(cotangent.astype(jnp.float32), axis=0)
     dense_grad = contract_rows(attended_low, cotangent)
     down_grad = contract_rows(hidden_low, cotangent)
@@ -178,51 +208,49 @@
     qkv_grad = contract_rows(attn_entry, joined_grad)
     qkv_bias_grad = jnp.sum(joined_grad.astype(jnp.float32), axis=0)
     attn_entry_grad = contract_cols(joined_grad, qkv_weight)
-    attn_summed, mlp_summed = lax.psum((attn_entry_grad, mlp_entry_grad), "mp")
-    attn_parts = attn_back(attn_summed)
-    mlp_parts = mlp_back(mlp_summed)
-    input_grad = cotangent.astype(jnp.float32) + attn_parts[0] + mlp_parts[0]
-    norm_grads = (attn_parts[1], attn_parts[2], mlp_parts[1], mlp_parts[2])
-    every_sum = (
-        lax.psum_scatter(qkv_grad, "dp", scatter_dimension=0, tiled=True),
-        lax.psum_scatter(qkv_bias_grad, "dp", scatter_dimension=0, tiled=True),
-        lax.psum_scatter(dense_grad, "dp", scatter_dimension=1, tiled=True),
-        lax.psum_scatter(up_grad, "dp", scatter_dimension=0, tiled=True),
-        lax.psum_scatter(up_bias_grad, "dp", scatter_dimension=0, tiled=True),
-        lax.psum_scatter(down_grad, "dp", scatter_dimension=1, tiled=True),
-        lax.psum_scatter(out_bias_grad, "dp", scatter_dimension=0, tiled=True),
-        lax.psum_scatter(norm_grads[0], "dp", scatter_dimension=0, tiled=True),
-        lax.psum_scatter(norm_grads[1], "dp", scatter_dimension=0, tiled=True),
-        lax.psum_scatter(norm_grads[2], "dp", scatter_dimension=0, tiled=True),
-        lax.psum_scatter(norm_grads[3], "dp", scatter_dimension=0, tiled=True),
-    )
-    (
-        qkv_total,
-        qkv_bias_total,
-        dense_total,
-        up_total,
-        up_bias_total,
-        down_total,
-        out_bias_total,
-        gain_first,
-        shift_first,
-        gain_second,
-        shift_second,
-    ) = every_sum
+
+    both = attn_entry_grad * attn_gain + mlp_entry_grad * mlp_gain
+    norm_grads = jnp.stack(
+        [
+            jnp.sum(attn_entry_grad * xhat, axis=0),
+            jnp.sum(attn_entry_grad, axis=0),
+            jnp.sum(mlp_entry_grad * xhat, axis=0),
+            jnp.sum(mlp_entry_grad, axis=0),
+        ]
+    )
+    grads_in = []
+    for first in range(0, count, chunk):
+        rows = slice(first, first + chunk)
+        entry = line_sum(both[rows], mp_size)
+        hat = xhat[rows]
+        inner = (
+            entry
+            - jnp.mean(entry, axis=-1, keepdims=True)
+            - hat * jnp.mean(entry * hat, axis=-1, keepdims=True)
+        )
+        grads_in.append(
+            (cotangent[rows].astype(jnp.float32) + factor[rows] * inner).astype(jnp.bfloat16)
+        )
+    input_grad = jnp.concatenate(grads_in)
+
+    def scattered(array, dimension):
+        return lax.psum_scatter(array, "dp", scatter_dimension=dimension, tiled=True)
+
+    norm_total = lax.psum(scattered(norm_grads, 1), "mp")
     return (
         layer_output,
-        input_grad.astype(jnp.bfloat16),
-        gain_first,
-        shift_first,
-        gain_second,
-        shift_second,
-        qkv_total,
-        qkv_bias_total,
-        dense_total,
-        up_total,
-        up_bias_total,
-        down_total,
-        out_bias_total,
+        input_grad,
+        norm_total[0],
+        norm_total[1],
+        norm_total[2],
+        norm_total[3],
+        scattered(qkv_grad, 0),
+        scattered(qkv_bias_grad, 0),
+        scattered(dense_grad, 1),
+        scattered(up_grad, 0),
+        scattered(up_bias_grad, 0),
+        scattered(down_grad, 1),
+        scattered(out_bias_grad, 0),
     )
 
 
@@ -259,5 +287,5 @@
         P("dp"),
     )
     return jax.shard_map(
-        per_device, mesh=mesh, in_specs=in_specs, out_specs=out_specs, check_vma=False
-    )
+        functools.partial(per_device, mesh.shape["mp"]), mesh=mesh, in_specs=in_specs, out_specs=out_specs, check_vma=False
+    )

time: 1140 us -> 1230 us (1.079)
  waiting for transfers between devices: 781 us -> 596 us
  starting transfers between devices: 0.68 us -> 96.2 us
  blocking collectives: 24.6 us -> 103 us
  matrix products: 182 us -> 226 us
  other arithmetic: 63.1 us -> 104 us
    psum x1 -> x0, waiting for transfers between devices: 781 us -> none  [per_device(): branch = lax.psum(partial_sum, 'mp')]
    ppermute x0 -> x48, waiting for transfers between devices: none -> 596 us  [the longest x16 368 us: line_sum(): came = lax.ppermute(total, 'mp', pairs)]
    ppermute x0 -> x48, starting transfers between devices: none -> 95.9 us  [the longest x16 59.2 us: line_sum(): total = total + lax.ppermute(total, 'mp', pairs)]
    psum x0 -> x1, blocking collectives: none -> 81.1 us  [per_device(): norm_total = lax.psum(scattered(norm_grads, 1), 'mp')]
    add x0 -> x25, other arithmetic: none -> 45.8 us  [the longest x9 25.2 us: line_sum(): total = total + lax.ppermute(total, 'mp', pairs)]
    dot_general x3 -> x24, matrix products: 30 us -> 74.3 us  [the longest x8 37.2 us: per_device(): jnp.dot(mlp_entry[rows], up_weight, preferred_element_type=jnp.float32)]
    unnamed x4 -> x22, other arithmetic: 0.01 us -> 19.1 us
    reduce_sum x4 -> x3, other arithmetic: 22.5 us -> 10 us  [the longest x1 5.82 us: per_device(): jnp.mean(entry * hat, axis=-1, keepdims=True)]
  transfers between devices with their start and end apart: 5 -> 53, of which waited for: 1 -> 25; matrix products, arithmetic and copies ran while one was open for 8% -> 14% of each run, Pallas kernels for 0% -> 0%
where the time goes in v1:
time: 1230 us; the launch traced here: 1220 us
  waiting for transfers between devices  596 us (48%)
  matrix products  226 us (18%)
  other arithmetic  104 us (8%)
  blocking collectives  103 us (8%)
  starting transfers between devices  96.2 us (8%)
  local copies, waits for them, and re-layouts  68.9 us (6%)
  between operations  17.5 us (1%)
    ppermute x16, waiting for transfers between devices, line_sum(): came = lax.ppermute(total, 'mp', pairs)  368 us
    ppermute x16, waiting for transfers between devices, line_sum(): total = total + lax.ppermute(total, 'mp', pairs)  228 us
    psum x1, blocking collectives, per_device(): norm_total = lax.psum(scattered(norm_grads, 1), 'mp')  81.1 us
    dot_general x4, matrix products, contract_cols(): lax.dot_general(left, right, (((1,), (1,)), ((), ())), preferred_element_...  67 us
    ppermute x16, starting transfers between devices, line_sum(): total = total + lax.ppermute(total, 'mp', pairs)  59.2 us
    dot_general x4, matrix products, contract_rows(): lax.dot_general(left, right, (((0,), (0,)), ((), ())), preferred_element_...  48.7 us
    dot_general x8, matrix products, per_device(): jnp.dot(mlp_entry[rows], up_weight, preferred_element_type=jnp.float32)  37.2 us
    unnamed x269, local copies, waits for them, and re-layouts  28.3 us
  transfers between devices with their start and end apart: 53, of which 25 were waited for; matrix products, arithmetic and copies ran while one was open for 14% of the time, Pallas kernels for 0%

profile of v1, /device:TPU:0, one launch (start us, length us, event | category | flops | bytes accessed | tf_op | source)
XLA Modules:
  0.0 1219.1 jit_solution(2599954482572313863)
XLA Ops:
  74.0 33.6 %while.29 = (s32[]{:T(128)}, f32[1024,2,256]{0,2,1:T(8,128)}, f32[1024,2,256]{0,2,1:T(8,128)}, f32[2,512,2,256]{3,1,0,2:T(8,128)}, s32[2]{0:T(128)S(1)}, /*index...) while((s32[]{:T(128)}, f32[1024,2,256]{0,2,1:T(8,128)}, ...), condition=%wide.region_11.12_spmd.clone, body=%wide.region_9.11_spmd.clone.sunk | while | flops 2704539136 | bytes 111192624 | solution.py:202
  173.2 29.3 %convert_reduce_fusion.1 = (f32[2048]{0:T(1024)}, bf16[1024,2048]{1,0:T(8,128)(2,1)}) fusion(f32[1024,2048]{1,0:T(8,128)S(1)} %constant_dynamic-update-slice_fusion, bf16[1024,2048]{1,0:T(8,128)(2,1)S(1)} %copy-done.6, bf16[2048,2048]{1,0:T(8,128)(2,1)S(1)} %bitcast.144), kind=kOutput, calls=%fused_computation.56 | convolution fusion | flops 8745121792 | bytes 25174016 | tf_op jit(solution)/shard_map/dot_general | solution.py:44
  215.6 19.2 %multiply_reduce_fusion.2 = (f32[2048]{0:T(1024)S(1)}, f32[2048]{0:T(1024)S(1)}, f32[2048]{0:T(1024)S(1)}, f32[2048]{0:T(1024)S(1)}, f32[1024,2048]{1,0:T(8,128)}, /*index=5*/f32[1024,2048]{1,0:T(8,128)}) fusion(bf16[1024,2048]{1,0:T(8,128)(2,1)} %param.18, f32[1024]{0:T(1024)S(1)} %copy-done.107, f32[1024]{0:T(1024)S(1)} %copy-done.109, ...), kind=kOutput, calls=%fused_computation.58 | convolution fusion | flops 6467608576 | bytes 38854656 | tf_op jit(solution)/shard_map/dot_general | solution.py:44
  358.1 18.0 %collective-permute-done.9 = f32[128,2048]{1,0:T(8,128)} collective-permute-done((f32[128,2048]{1,0:T(8,128)}, f32[128,2048]{1,0:T(8,128)}, u32[]{:S(2)}, u32[]{:S(2)}) %collective-permute-start.9) | collective-permute-done | bytes 1048608 | tf_op jit(solution)/shard_map/ppermute | solution.py:59
  380.6 17.9 %collective-permute-done.12 = f32[128,2048]{1,0:T(8,128)} collective-permute-done((f32[128,2048]{1,0:T(8,128)S(1)}, f32[128,2048]{1,0:T(8,128)}, u32[]{:S(2)}, u32[]{:S(2)}) %collective-permute-start.12) | collective-permute-done | bytes 1048608 | tf_op jit(solution)/shard_map/ppermute | solution.py:59
  403.1 17.9 %collective-permute-done.15 = f32[128,2048]{1,0:T(8,128)S(1)} collective-permute-done((f32[128,2048]{1,0:T(8,128)S(1)}, f32[128,2048]{1,0:T(8,128)S(1)}, u32[]{:S(2)}, u32[]{:S(2)}) %collective-permute-start.15) | collective-permute-done | bytes 1048608 | tf_op jit(solution)/shard_map/ppermute | solution.py:59
  425.5 18.0 %collective-permute-done.18 = f32[128,2048]{1,0:T(8,128)S(1)} collective-permute-done((f32[128,2048]{1,0:T(8,128)S(1)}, f32[128,2048]{1,0:T(8,128)S(1)}, u32[]{:S(2)}, u32[]{:S(2)}) %collective-permute-start.18) | collective-permute-done | bytes 1048608 | tf_op jit(solution)/shard_map/ppermute | solution.py:59
  447.9 18.1 %collective-permute-done.24 = f32[128,2048]{1,0:T(8,128)S(1)} collective-permute-done((f32[128,2048]{1,0:T(8,128)}, f32[128,2048]{1,0:T(8,128)S(1)}, u32[]{:S(2)}, u32[]{:S(2)}) %collective-permute-start.24) | collective-permute-done | bytes 1048608 | tf_op jit(solution)/shard_map/ppermute | solution.py:59
  470.4 18.1 %collective-permute-done.45 = f32[128,2048]{1,0:T(8,128)S(1)} collective-permute-done((f32[128,2048]{1,0:T(8,128)}, f32[128,2048]{1,0:T(8,128)S(1)}, u32[]{:S(2)}, u32[]{:S(2)}) %collective-permute-start.45) | collective-permute-done | bytes 1048608 | tf_op jit(solution)/shard_map/ppermute | solution.py:59
  492.9 18.1 %collective-permute-done.42 = f32[128,2048]{1,0:T(8,128)S(1)} collective-permute-done((f32[128,2048]{1,0:T(8,128)}, f32[128,2048]{1,0:T(8,128)S(1)}, u32[]{:S(2)}, u32[]{:S(2)}) %collective-permute-start.42) | collective-permute-done | bytes 1048608 | tf_op jit(solution)/shard_map/ppermute | solution.py:59
  557.6 20.7 %collective-permute-done.33 = f32[128,2048]{1,0:T(8,128)S(1)} collective-permute-done((f32[128,2048]{1,0:T(8,128)S(1)}, f32[128,2048]{1,0:T(8,128)S(1)}, u32[]{:S(2)}, u32[]{:S(2)}) %collective-permute-start.33) | collective-permute-done | bytes 1048608 | tf_op jit(solution)/shard_map/ppermute | solution.py:59
  581.7 19.1 %collective-permute-done.30 = f32[128,2048]{1,0:T(8,128)S(1)} collective-permute-done((f32[128,2048]{1,0:T(8,128)S(1)}, f32[128,2048]{1,0:T(8,128)S(1)}, u32[]{:S(2)}, u32[]{:S(2)}) %collective-permute-start.30) | collective-permute-done | bytes 1048608 | tf_op jit(solution)/shard_map/ppermute | solution.py:59
  604.3 18.9 %collective-permute-done.27 = f32[128,2048]{1,0:T(8,128)S(1)} collective-permute-done((f32[128,2048]{1,0:T(8,128)S(1)}, f32[128,2048]{1,0:T(8,128)S(1)}, u32[]{:S(2)}, u32[]{:S(2)}) %collective-permute-start.27) | collective-permute-done | bytes 1048608 | tf_op jit(solution)/shard_map/ppermute | solution.py:59
  672.8 180.4 %collective-permute-done.26 = f32[128,2048]{1,0:T(8,128)S(1)} collective-permute-done((f32[128,2048]{1,0:T(8,128)S(1)}, f32[128,2048]{1,0:T(8,128)S(1)}, u32[]{:S(2)}, u32[]{:S(2)}) %collective-permute-start.26) | collective-permute-done | bytes 1048608 | tf_op jit(solution)/shard_map/ppermute | solution.py:63
  854.5 21.2 %collective-permute-done.29 = f32[128,2048]{1,0:T(8,128)S(1)} collective-permute-done((f32[128,2048]{1,0:T(8,128)S(1)}, f32[128,2048]{1,0:T(8,128)S(1)}, u32[]{:S(2)}, u32[]{:S(2)}) %collective-permute-start.29) | collective-permute-done | bytes 1048608 | tf_op jit(solution)/shard_map/ppermute | solution.py:63
  877.0 21.2 %collective-permute-done.32 = f32[128,2048]{1,0:T(8,128)S(1)} collective-permute-done((f32[128,2048]{1,0:T(8,128)S(1)}, f32[128,2048]{1,0:T(8,128)S(1)}, u32[]{:S(2)}, u32[]{:S(2)}) %collective-permute-start.32) | collective-permute-done | bytes 1048608 | tf_op jit(solution)/shard_map/ppermute | solution.py:63
  908.7 22.4 %all-reduce.11 = (f32[1536]{0:T(1024)S(1)}, f32[2048]{0:T(1024)S(1)}, f32[2048]{0:T(1024)S(1)}) all-reduce(f32[1536]{0:T(1024)S(1)} %reduce_sum.288, f32[2048]{0:T(1024)S(1)} %copy-done.114, f32[2048]{0:T(1024)S(1)} %convert_reduce_fusion), channel_id=4, replica_groups=mesh['dp'=8,'mp'=4] {'dp'}, use_global_device_ids=true, to_apply=%region_36.37.clone | all-reduce | flops 5632 | bytes 45056
  933.9 81.1 %psum.7 = f32[4,256]{1,0:T(4,128)S(1)} all-reduce(f32[4,256]{1,0:T(4,128)S(1)} %copy.90), channel_id=1, replica_groups=mesh['dp'=8,'mp'=4] {'mp'}, use_global_device_ids=true, to_apply=%region_33.34 | all-reduce | flops 1024 | bytes 8192 | tf_op jit(solution)/shard_map/psum | solution.py:239
  1062.5 18.6 %collective-permute-done.5 = f32[128,2048]{1,0:T(8,128)} collective-permute-done((f32[128,2048]{1,0:T(8,128)}, f32[128,2048]{1,0:T(8,128)}, u32[]{:S(2)}, u32[]{:S(2)}) %collective-permute-start.5) | collective-permute-done | bytes 1048608 | tf_op jit(solution)/shard_map/ppermute | solution.py:63
  1085.6 17.9 %collective-permute-done.8 = f32[128,2048]{1,0:T(8,128)} collective-permute-done((f32[128,2048]{1,0:T(8,128)}, f32[128,2048]{1,0:T(8,128)}, u32[]{:S(2)}, u32[]{:S(2)}) %collective-permute-start.8) | collective-permute-done | bytes 1048608 | tf_op jit(solution)/shard_map/ppermute | solution.py:63
  1107.4 18.6 %collective-permute-done.11 = f32[128,2048]{1,0:T(8,128)} collective-permute-done((f32[128,2048]{1,0:T(8,128)}, f32[128,2048]{1,0:T(8,128)}, u32[]{:S(2)}, u32[]{:S(2)}) %collective-permute-start.11) | collective-permute-done | bytes 1048608 | tf_op jit(solution)/shard_map/ppermute | solution.py:63
  1129.0 19.5 %collective-permute-done.14 = f32[128,2048]{1,0:T(8,128)} collective-permute-done((f32[128,2048]{1,0:T(8,128)}, f32[128,2048]{1,0:T(8,128)}, u32[]{:S(2)}, u32[]{:S(2)}) %collective-permute-start.14) | collective-permute-done | bytes 1048608 | tf_op jit(solution)/shard_map/ppermute | solution.py:63
  1150.8 20.1 %collective-permute-done.17 = f32[128,2048]{1,0:T(8,128)S(1)} collective-permute-done((f32[128,2048]{1,0:T(8,128)S(1)}, f32[128,2048]{1,0:T(8,128)S(1)}, u32[]{:S(2)}, u32[]{:S(2)}) %collective-permute-start.17) | collective-permute-done | bytes 1048608 | tf_op jit(solution)/shard_map/ppermute | solution.py:63
  1172.6 20.8 %collective-permute-done.20 = f32[128,2048]{1,0:T(8,128)S(1)} collective-permute-done((f32[128,2048]{1,0:T(8,128)S(1)}, f32[128,2048]{1,0:T(8,128)S(1)}, u32[]{:S(2)}, u32[]{:S(2)}) %collective-permute-start.20) | collective-permute-done | bytes 1048608 | tf_op jit(solution)/shard_map/ppermute | solution.py:63
  (587 shorter events, 535.3 us)
Async XLA Ops:
  7.2 925.8 %reduce-scatter.16.cloned.1.call-start = ((), (), s32[]{:S(2)}) async-start(), calls=%async_computation.9 | async-start | bytes 1179648
  236.2 976.2 %reduce-scatter.10.cloned.1.call-start = ((), (), s32[]{:S(2)}) async-start(), calls=%async_computation.6 | async-start | bytes 4718592 | tf_op jit(solution)/shard_map/reduce_scatter | solution.py:237
  242.8 969.5 %reduce-scatter.8.cloned.1.call-start = ((), (), s32[]{:S(2)}) async-start(), calls=%async_computation.5 | async-start | bytes 14155776 | tf_op jit(solution)/shard_map/reduce_scatter | solution.py:237
  258.2 954.1 %reduce-scatter.12.cloned.1.call-start = ((), (), s32[]{:S(2)}) async-start(), calls=%async_computation.7 | async-start | bytes 18874368 | tf_op jit(solution)/shard_map/reduce_scatter | solution.py:237
  273.7 938.6 %reduce-scatter.14.cloned.1.call-start = ((), (), s32[]{:S(2)}) async-start(), calls=%async_computation.8 | async-start | bytes 18874368 | tf_op jit(solution)/shard_map/reduce_scatter | solution.py:237
  353.7 112.4 %collective-permute-start.24 = (f32[128,2048]{1,0:T(8,128)}, f32[128,2048]{1,0:T(8,128)S(1)}, u32[]{:S(2)}, u32[]{:S(2)}) collective-permute-start(f32[128,2048]{1,0:T(8,128)} %get-tuple-element.368), channel_id=1, source_target_pairs={{0,1},{3,2},{4,5},{7,6},{8,9},{11,10},{12,13},{15,14},{16,17},{19,... | collective-permute-start | bytes 3145736 | tf_op jit(solution)/shard_map/ppermute | solution.py:59
  376.2 112.4 %collective-permute-start.45 = (f32[128,2048]{1,0:T(8,128)}, f32[128,2048]{1,0:T(8,128)S(1)}, u32[]{:S(2)}, u32[]{:S(2)}) collective-permute-start(f32[128,2048]{1,0:T(8,128)} %get-tuple-element.369), channel_id=1, source_target_pairs={{0,1},{3,2},{4,5},{7,6},{8,9},{11,10},{12,13},{15,14},{16,17},{19,... | collective-permute-start | bytes 3145736 | tf_op jit(solution)/shard_map/ppermute | solution.py:59
  398.5 112.5 %collective-permute-start.42 = (f32[128,2048]{1,0:T(8,128)}, f32[128,2048]{1,0:T(8,128)S(1)}, u32[]{:S(2)}, u32[]{:S(2)}) collective-permute-start(f32[128,2048]{1,0:T(8,128)} %get-tuple-element.370), channel_id=1, source_target_pairs={{0,1},{3,2},{4,5},{7,6},{8,9},{11,10},{12,13},{15,14},{16,17},{19,... | collective-permute-start | bytes 3145736 | tf_op jit(solution)/shard_map/ppermute | solution.py:59
  421.0 112.5 %collective-permute-start.39 = (f32[128,2048]{1,0:T(8,128)}, f32[128,2048]{1,0:T(8,128)S(1)}, u32[]{:S(2)}, u32[]{:S(2)}) collective-permute-start(f32[128,2048]{1,0:T(8,128)} %get-tuple-element.371), channel_id=1, source_target_pairs={{0,1},{3,2},{4,5},{7,6},{8,9},{11,10},{12,13},{15,14},{16,17},{19,... | collective-permute-start | bytes 3145736 | tf_op jit(solution)/shard_map/ppermute | solution.py:59
  443.5 112.5 %collective-permute-start.36 = (f32[128,2048]{1,0:T(8,128)}, f32[128,2048]{1,0:T(8,128)S(1)}, u32[]{:S(2)}, u32[]{:S(2)}) collective-permute-start(f32[128,2048]{1,0:T(8,128)} %get-tuple-element.372), channel_id=1, source_target_pairs={{0,1},{3,2},{4,5},{7,6},{8,9},{11,10},{12,13},{15,14},{16,17},{19,... | collective-permute-start | bytes 3145736 | tf_op jit(solution)/shard_map/ppermute | solution.py:59
  466.1 112.2 %collective-permute-start.33 = (f32[128,2048]{1,0:T(8,128)S(1)}, f32[128,2048]{1,0:T(8,128)S(1)}, u32[]{:S(2)}, u32[]{:S(2)}) collective-permute-start(f32[128,2048]{1,0:T(8,128)S(1)} %copy-done.86), channel_id=1, source_target_pairs={{0,1},{3,2},{4,5},{7,6},{8,9},{11,10},{12,13},{15,14},{16,17},{19,... | collective-permute-start | bytes 3145736 | tf_op jit(solution)/shard_map/ppermute | solution.py:59
  488.5 112.2 %collective-permute-start.30 = (f32[128,2048]{1,0:T(8,128)S(1)}, f32[128,2048]{1,0:T(8,128)S(1)}, u32[]{:S(2)}, u32[]{:S(2)}) collective-permute-start(f32[128,2048]{1,0:T(8,128)S(1)} %copy-done.84), channel_id=1, source_target_pairs={{0,1},{3,2},{4,5},{7,6},{8,9},{11,10},{12,13},{15,14},{16,17},{19,... | collective-permute-start | bytes 3145736 | tf_op jit(solution)/shard_map/ppermute | solution.py:59
  511.0 112.2 %collective-permute-start.27 = (f32[128,2048]{1,0:T(8,128)S(1)}, f32[128,2048]{1,0:T(8,128)S(1)}, u32[]{:S(2)}, u32[]{:S(2)}) collective-permute-start(f32[128,2048]{1,0:T(8,128)S(1)} %copy-done.81), channel_id=1, source_target_pairs={{0,1},{3,2},{4,5},{7,6},{8,9},{11,10},{12,13},{15,14},{16,17},{19,... | collective-permute-start | bytes 3145736 | tf_op jit(solution)/shard_map/ppermute | solution.py:59
  660.5 192.7 %collective-permute-start.26 = (f32[128,2048]{1,0:T(8,128)S(1)}, f32[128,2048]{1,0:T(8,128)S(1)}, u32[]{:S(2)}, u32[]{:S(2)}) collective-permute-start(f32[128,2048]{1,0:T(8,128)S(1)} %add.470), channel_id=1, source_target_pairs={{1,0},{2,3},{5,4},{6,7},{9,8},{10,11},{13,12},{14,15},{17,16},{18,... | collective-permute-start | bytes 3145736 | tf_op jit(solution)/shard_map/ppermute | solution.py:63
  661.9 213.8 %collective-permute-start.29 = (f32[128,2048]{1,0:T(8,128)S(1)}, f32[128,2048]{1,0:T(8,128)S(1)}, u32[]{:S(2)}, u32[]{:S(2)}) collective-permute-start(f32[128,2048]{1,0:T(8,128)S(1)} %add.473), channel_id=1, source_target_pairs={{1,0},{2,3},{5,4},{6,7},{9,8},{10,11},{13,12},{14,15},{17,16},{18,... | collective-permute-start | bytes 3145736 | tf_op jit(solution)/shard_map/ppermute | solution.py:63
  663.2 234.9 %collective-permute-start.32 = (f32[128,2048]{1,0:T(8,128)S(1)}, f32[128,2048]{1,0:T(8,128)S(1)}, u32[]{:S(2)}, u32[]{:S(2)}) collective-permute-start(f32[128,2048]{1,0:T(8,128)S(1)} %add.476), channel_id=1, source_target_pairs={{1,0},{2,3},{5,4},{6,7},{9,8},{10,11},{13,12},{14,15},{17,16},{18,... | collective-permute-start | bytes 3145736 | tf_op jit(solution)/shard_map/ppermute | solution.py:63
  670.1 360.2 %collective-permute-start.35 = (f32[128,2048]{1,0:T(8,128)}, f32[128,2048]{1,0:T(8,128)}, u32[]{:S(2)}, u32[]{:S(2)}) collective-permute-start(f32[128,2048]{1,0:T(8,128)} %add.479), channel_id=1, source_target_pairs={{1,0},{2,3},{5,4},{6,7},{9,8},{10,11},{13,12},{14,15},{17,16},{18,... | collective-permute-start | bytes 3145736 | tf_op jit(solution)/shard_map/ppermute | solution.py:63
  671.5 360.2 %collective-permute-start.38 = (f32[128,2048]{1,0:T(8,128)}, f32[128,2048]{1,0:T(8,128)}, u32[]{:S(2)}, u32[]{:S(2)}) collective-permute-start(f32[128,2048]{1,0:T(8,128)} %add.482), channel_id=1, source_target_pairs={{1,0},{2,3},{5,4},{6,7},{9,8},{10,11},{13,12},{14,15},{17,16},{18,... | collective-permute-start | bytes 3145736 | tf_op jit(solution)/shard_map/ppermute | solution.py:63
  853.2 179.7 %collective-permute-start.41 = (f32[128,2048]{1,0:T(8,128)}, f32[128,2048]{1,0:T(8,128)}, u32[]{:S(2)}, u32[]{:S(2)}) collective-permute-start(f32[128,2048]{1,0:T(8,128)} %add.485), channel_id=1, source_target_pairs={{1,0},{2,3},{5,4},{6,7},{9,8},{10,11},{13,12},{14,15},{17,16},{18,... | collective-permute-start | bytes 3145736 | tf_op jit(solution)/shard_map/ppermute | solution.py:63
  875.7 158.6 %collective-permute-start.44 = (f32[128,2048]{1,0:T(8,128)}, f32[128,2048]{1,0:T(8,128)}, u32[]{:S(2)}, u32[]{:S(2)}) collective-permute-start(f32[128,2048]{1,0:T(8,128)} %add.488), channel_id=1, source_target_pairs={{1,0},{2,3},{5,4},{6,7},{9,8},{10,11},{13,12},{14,15},{17,16},{18,... | collective-permute-start | bytes 3145736 | tf_op jit(solution)/shard_map/ppermute | solution.py:63
  898.1 137.4 %collective-permute-start.47 = (f32[128,2048]{1,0:T(8,128)}, f32[128,2048]{1,0:T(8,128)}, u32[]{:S(2)}, u32[]{:S(2)}) collective-permute-start(f32[128,2048]{1,0:T(8,128)} %add.491), channel_id=1, source_target_pairs={{1,0},{2,3},{5,4},{6,7},{9,8},{10,11},{13,12},{14,15},{17,16},{18,... | collective-permute-start | bytes 3145736 | tf_op jit(solution)/shard_map/ppermute | solution.py:63
  1035.6 113.0 %collective-permute-start.14 = (f32[128,2048]{1,0:T(8,128)}, f32[128,2048]{1,0:T(8,128)}, u32[]{:S(2)}, u32[]{:S(2)}) collective-permute-start(f32[128,2048]{1,0:T(8,128)} %add.447), channel_id=1, source_target_pairs={{1,0},{2,3},{5,4},{6,7},{9,8},{10,11},{13,12},{14,15},{17,16},{18,... | collective-permute-start | bytes 3145736 | tf_op jit(solution)/shard_map/ppermute | solution.py:63
  1058.6 112.2 %collective-permute-start.17 = (f32[128,2048]{1,0:T(8,128)S(1)}, f32[128,2048]{1,0:T(8,128)S(1)}, u32[]{:S(2)}, u32[]{:S(2)}) collective-permute-start(f32[128,2048]{1,0:T(8,128)S(1)} %copy-done.50), channel_id=1, source_target_pairs={{1,0},{2,3},{5,4},{6,7},{9,8},{10,11},{13,12},{14,15},{17,16},{18,... | collective-permute-start | bytes 3145736 | tf_op jit(solution)/shard_map/ppermute | solution.py:63
  1081.1 112.2 %collective-permute-start.20 = (f32[128,2048]{1,0:T(8,128)S(1)}, f32[128,2048]{1,0:T(8,128)S(1)}, u32[]{:S(2)}, u32[]{:S(2)}) collective-permute-start(f32[128,2048]{1,0:T(8,128)S(1)} %copy-done.49), channel_id=1, source_target_pairs={{1,0},{2,3},{5,4},{6,7},{9,8},{10,11},{13,12},{14,15},{17,16},{18,... | collective-permute-start | bytes 3145736 | tf_op jit(solution)/shard_map/ppermute | solution.py:63
  (176 other events, 4689.7 us)
Sparse Core Ops, SparseCore 0:
  236.3 38.7 reduce-scatter.15
  279.0 51.2 reduce-scatter.9
  334.8 92.4 reduce-scatter.7
  431.6 115.9 reduce-scatter.11
  552.0 115.8 reduce-scatter.13

commit v2 on v1

--- a/solution.py
+++ b/solution.py
@@ -4,6 +4,8 @@
 import jax
 import jax.numpy as jnp
 from jax import lax
+from jax.experimental import pallas as pl
+from jax.experimental.pallas import tpu as pltpu
 from jax.sharding import PartitionSpec as P
 
 HEAD_DIM = 256
@@ -46,26 +48,351 @@
     )
 
 
-def line_sum(part, size):
-    if size == 1:
-        return part
-    if size % 2:
-        return lax.psum(part, "mp")
+MESH = pl.DeviceIdType.MESH
+ROWS = 64
+CHUNK = 256
+
+
+def gelu_parts(v):
+    cdf = 0.5 + 0.5 * lax.erf(v * math.sqrt(0.5))
+    return v * cdf, cdf + v * jnp.exp(-0.5 * v * v) * (1.0 / math.sqrt(2.0 * math.pi))
+
+
+def layer_kernel(
+    size,
+    tokens,
+    cotangent,
+    mlp_entry,
+    attended,
+    up_weight,
+    down_weight,
+    dense_weight,
+    up_bias,
+    out_bias,
+    layer_out,
+    hidden_out,
+    hidden_grad_out,
+    part,
+    from_outer,
+    from_inner,
+    token_rows,
+    out_rows,
+    send_in,
+    send_out,
+    recv_outer,
+    recv_inner,
+    row_sems,
+    out_sems,
+):
+    count, width = tokens.shape
+    inner_width = up_weight.shape[1]
+    messages = count // ROWS
+    half = size // 2
     index = lax.axis_index("mp")
-    half = size // 2
-    total = part
-    for hop in range(half - 1):
-        pairs = [(hop, hop + 1), (size - 1 - hop, size - 2 - hop)]
-        total = total + lax.ppermute(total, "mp", pairs)
-    total = total + lax.ppermute(total, "mp", [(half - 1, half), (half, half - 1)])
-    for hop in reversed(range(half - 1)):
-        pairs = [(hop + 1, hop), (size - 2 - hop, size - 1 - hop)]
-        came = lax.ppermute(total, "mp", pairs)
-        total = jnp.where((index == hop) | (index == size - 1 - hop), came, total)
-    return total
-
-
-CHUNK = 128
+    upper = index // half
+    level = index * (1 - upper) + (size - 1 - index) * upper
+    inner = index + 1 - 2 * upper
+    outer = index - 1 + 2 * upper
+    lag = half - level
+    is_end = level == 0
+    is_middle = level == half - 1
+
+    barrier = pltpu.get_barrier_semaphore()
+    pl.semaphore_signal(barrier, inc=1, device_id={"mp": inner}, device_id_type=MESH)
+
+    @pl.when(level > 0)
+    def _():
+        pl.semaphore_signal(barrier, inc=1, device_id={"mp": outer}, device_id_type=MESH)
+        pl.semaphore_wait(barrier, 2)
+
+    @pl.when(level == 0)
+    def _():
+        pl.semaphore_wait(barrier, 1)
+
+    def rows_of(ref, k):
+        return ref.at[pl.ds(pl.multiple_of(lax.rem(k, messages) * ROWS, ROWS), ROWS)]
+
+    def to_inner(k, landing, sem):
+        return pltpu.make_async_remote_copy(
+            src_ref=rows_of(part, k),
+            dst_ref=rows_of(landing, k),
+            send_sem=send_in.at[k],
+            recv_sem=sem.at[k],
+            device_id={"mp": inner},
+            device_id_type=MESH,
+        )
+
+    def to_outer(k, source):
+        return pltpu.make_async_remote_copy(
+            src_ref=rows_of(source, k),
+            dst_ref=rows_of(from_inner, k),
+            send_sem=send_out.at[k],
+            recv_sem=recv_inner.at[k],
+            device_id={"mp": outer},
+            device_id_type=MESH,
+        )
+
+    def send_inward(k):
+        @pl.when(is_middle)
+        def _():
+            to_inner(k, from_inner, recv_inner).start()
+
+        if half > 1:
+
+            @pl.when(level < half - 1)
+            def _():
+                to_inner(k, from_outer, recv_outer).start()
+
+    def emit(k):
+        @pl.when(is_end)
+        def _():
+            send_inward(k)
+
+    def load_rows(k):
+        return pltpu.make_async_copy(
+            tokens.at[pl.ds(pl.multiple_of(k * ROWS, ROWS), ROWS)],
+            token_rows.at[lax.rem(k, 2)],
+            row_sems.at[lax.rem(k, 2)],
+        )
+
+    def store_rows(k):
+        return pltpu.make_async_copy(
+            out_rows.at[lax.rem(k, 2)],
+            layer_out.at[pl.ds(pl.multiple_of(k * ROWS, ROWS), ROWS)],
+            out_sems.at[lax.rem(k, 2)],
+        )
+
+    def finish(k, source):
+        total = rows_of(source, k)[...]
+        out_rows[lax.rem(k, 2)] = (
+            token_rows[lax.rem(k, 2)].astype(jnp.float32) + total + out_bias[...]
+        ).astype(jnp.bfloat16)
+
+    def service(j):
+        @pl.when((level > 0) & (j < messages))
+        def _():
+            to_inner(j, from_outer, recv_outer).wait_recv()
+            rows_of(part, j)[...] += rows_of(from_outer, j)[...]
+            send_inward(j)
+
+        k = j - lag
+
+        @pl.when((k >= 0) & (k < messages))
+        def _():
+            to_outer(k, part).wait_recv()
+            to_inner(k, from_inner, recv_inner).wait_send()
+
+            @pl.when(k + 1 < messages)
+            def _():
+                load_rows(k + 1).start()
+
+            load_rows(k).wait()
+
+            @pl.when(k >= 2)
+            def _():
+                store_rows(k - 2).wait()
+
+            @pl.when(is_middle)
+            def _():
+                rows_of(part, k)[...] += rows_of(from_inner, k)[...]
+
+            if half > 1:
+
+                @pl.when(level > 0)
+                def _():
+                    @pl.when(k >= 1)
+                    def _():
+                        to_outer(k - 1, part).wait_send()
+
+                    @pl.when(is_middle)
+                    def _():
+                        to_outer(k, part).start()
+
+                    @pl.when(level < half - 1)
+                    def _():
+                        to_outer(k, from_inner).start()
+
+            @pl.when(is_middle)
+            def _():
+                finish(k, part)
+
+            if half > 1:
+
+                @pl.when(level < half - 1)
+                def _():
+                    finish(k, from_inner)
+
+            store_rows(k).start()
+
+    load_rows(0).start()
+
+    def feed_forward(up, down, dense, entry, cot, att, hid, hgrad, slope, w_sems, in_sems, h_sems):
+        up_copy = pltpu.make_async_copy(up_weight, up, w_sems.at[0])
+        down_copy = pltpu.make_async_copy(down_weight, down, w_sems.at[1])
+        dense_copy = pltpu.make_async_copy(dense_weight, dense, w_sems.at[2])
+        steps = count // CHUNK
+        tile = min(512, inner_width)
+        wide = min(512, width)
+
+        def loads(c):
+            slot = lax.rem(c, 2)
+            rows = pl.ds(pl.multiple_of(c * CHUNK, CHUNK), CHUNK)
+            return [
+                pltpu.make_async_copy(source.at[rows], target.at[slot], in_sems.at[slot, i])
+                for i, (source, target) in enumerate(
+                    ((mlp_entry, entry), (attended, att), (cotangent, cot))
+                )
+            ]
+
+        def stores(c):
+            rows = pl.ds(pl.multiple_of(c * CHUNK, CHUNK), CHUNK)
+            return [
+                pltpu.make_async_copy(hid, hidden_out.at[rows], h_sems.at[0]),
+                pltpu.make_async_copy(hgrad, hidden_grad_out.at[rows], h_sems.at[1]),
+            ]
+
+        for copy in loads(0):
+            copy.start()
+        up_copy.start()
+        down_copy.start()
+        dense_copy.start()
+
+        @pl.loop(0, steps)
+        def _(c):
+            slot = lax.rem(c, 2)
+
+            @pl.when(c + 1 < steps)
+            def _():
+                for copy in loads(c + 1):
+                    copy.start()
+
+            for copy in loads(c):
+                copy.wait()
+
+            @pl.when(c == 0)
+            def _():
+                up_copy.wait()
+
+            @pl.when(c > 0)
+            def _():
+                stores(c - 1)[0].wait()
+
+            @pl.loop(0, inner_width // tile)
+            def _(t):
+                cols = pl.ds(pl.multiple_of(t * tile, tile), tile)
+                pre = (
+                    jnp.dot(entry[slot], up[:, cols], preferred_element_type=jnp.float32)
+                    + up_bias[:, cols]
+                )
+                value, der = gelu_parts(pre)
+                hid[:, cols] = value.astype(jnp.bfloat16)
+                slope[:, cols] = der
+
+            @pl.when(c == 0)
+            def _():
+                down_copy.wait()
+                dense_copy.wait()
+
+            rows = pl.ds(pl.multiple_of(c * CHUNK, CHUNK), CHUNK)
+
+            @pl.loop(0, width // wide)
+            def _(t):
+                cols = pl.ds(pl.multiple_of(t * wide, wide), wide)
+                part[rows, cols] = jnp.dot(
+                    hid[...], down[:, cols], preferred_element_type=jnp.float32
+                ) + jnp.dot(att[slot], dense[:, cols], preferred_element_type=jnp.float32)
+
+            @pl.loop(0, CHUNK // ROWS)
+            def _(m):
+                emit(c * (CHUNK // ROWS) + m)
+
+            stores(c)[0].start()
+
+            @pl.when(c > 0)
+            def _():
+                stores(c - 1)[1].wait()
+
+            @pl.loop(0, inner_width // tile)
+            def _(t):
+                cols = pl.ds(pl.multiple_of(t * tile, tile), tile)
+                back = lax.dot_general(
+                    cot[slot],
+                    down[cols, :],
+                    (((1,), (1,)), ((), ())),
+                    preferred_element_type=jnp.float32,
+                )
+                hgrad[:, cols] = (back * slope[:, cols]).astype(jnp.bfloat16)
+
+            stores(c)[1].start()
+            service(c)
+
+        for copy in stores(steps - 1):
+            copy.wait()
+
+    pl.run_scoped(
+        feed_forward,
+        pltpu.VMEM(up_weight.shape, jnp.bfloat16),
+        pltpu.VMEM(down_weight.shape, jnp.bfloat16),
+        pltpu.VMEM(dense_weight.shape, jnp.bfloat16),
+        pltpu.VMEM((2, CHUNK, width), jnp.bfloat16),
+        pltpu.VMEM((2, CHUNK, width), jnp.bfloat16),
+        pltpu.VMEM((2, CHUNK, dense_weight.shape[0]), jnp.bfloat16),
+        pltpu.VMEM((CHUNK, inner_width), jnp.bfloat16),
+        pltpu.VMEM((CHUNK, inner_width), jnp.bfloat16),
+        pltpu.VMEM((CHUNK, inner_width), jnp.float32),
+        pltpu.SemaphoreType.DMA((3,)),
+        pltpu.SemaphoreType.DMA((2, 3)),
+        pltpu.SemaphoreType.DMA((2,)),
+    )
+
+    @pl.loop(count // CHUNK, messages + half)
+    def _(j):
+        service(j)
+
+    if half > 1:
+
+        @pl.when(level > 0)
+        def _():
+            to_outer(messages - 1, part).wait_send()
+
+    store_rows(messages - 2).wait()
+    store_rows(messages - 1).wait()
+
+
+def layer_call(size, tokens, cotangent, mlp_entry, attended, up, down, dense, up_bias, out_bias):
+    count, width = tokens.shape
+    messages = count // ROWS
+    anywhere = pl.BlockSpec(memory_space=pl.ANY)
+    vmem = pl.BlockSpec(memory_space=pltpu.VMEM)
+    return pl.pallas_call(
+        functools.partial(layer_kernel, size),
+        out_shape=(
+            jax.ShapeDtypeStruct((count, width), jnp.bfloat16),
+            jax.ShapeDtypeStruct((count, up.shape[1]), jnp.bfloat16),
+            jax.ShapeDtypeStruct((count, up.shape[1]), jnp.bfloat16),
+        ),
+        in_specs=[anywhere] * 7 + [vmem] * 2,
+        out_specs=(anywhere,) * 3,
+        scratch_shapes=[
+            pltpu.VMEM((count, width), jnp.float32),
+            pltpu.VMEM((count, width), jnp.float32),
+            pltpu.VMEM((count, width), jnp.float32),
+            pltpu.VMEM((2, ROWS, width), jnp.bfloat16),
+            pltpu.VMEM((2, ROWS, width), jnp.bfloat16),
+            pltpu.SemaphoreType.DMA((messages,)),
+            pltpu.SemaphoreType.DMA((messages,)),
+            pltpu.SemaphoreType.DMA((messages,)),
+            pltpu.SemaphoreType.DMA((messages,)),
+            pltpu.SemaphoreType.DMA((2,)),
+            pltpu.SemaphoreType.DMA((2,)),
+        ],
+        compiler_params=pltpu.CompilerParams(
+            collective_id=0, has_side_effects=True, vmem_limit_bytes=60 * 1024 * 1024
+        ),
+        cost_estimate=pl.CostEstimate(
+            flops=6 * count * width * up.shape[1], bytes_accessed=40 << 20, transcendentals=0
+        ),
+    )(tokens, cotangent, mlp_entry, attended, up, down, dense, up_bias[None], out_bias[None])
 
 
 def per_device(
@@ -137,28 +464,21 @@
     attended, log_total = lax.map(forward_block, jnp.arange(blocks, dtype=jnp.int32))
     attended_low = attended.reshape(count, width).astype(jnp.bfloat16)
 
-    chunk = min(CHUNK, count)
-    outputs, pres, hiddens = [], [], []
-    for first in range(0, count, chunk):
-        rows = slice(first, first + chunk)
-        pre = jnp.dot(mlp_entry[rows], up_weight, preferred_element_type=jnp.float32) + up_bias
-        hidden = jax.nn.gelu(pre, approximate=False).astype(jnp.bfloat16)
-        part = jnp.dot(
-            attended_low[rows], dense_weight, preferred_element_type=jnp.float32
-        ) + jnp.dot(hidden, down_weight, preferred_element_type=jnp.float32)
-        branch = line_sum(part, mp_size)
-        outputs.append((inputs[rows] + branch + out_bias).astype(jnp.bfloat16))
-        pres.append(pre)
-        hiddens.append(hidden)
-    layer_output = jnp.concatenate(outputs)
-    hidden_pre = jnp.concatenate(pres)
-    hidden_low = jnp.concatenate(hiddens)
-    _, gelu_back = jax.vjp(lambda field: jax.nn.gelu(field, approximate=False), hidden_pre)
-
+    layer_output, hidden_low, hidden_grad = layer_call(
+        mp_size,
+        tokens,
+        cotangent,
+        mlp_entry,
+        attended_low,
+        up_weight,
+        down_weight,
+        dense_weight,
+        up_bias,
+        out_bias,
+    )
     out_bias_grad = jnp.sum(cotangent.astype(jnp.float32), axis=0)
     dense_grad = contract_rows(attended_low, cotangent)
     down_grad = contract_rows(hidden_low, cotangent)
-    hidden_grad = gelu_back(contract_cols(cotangent, down_weight))[0].astype(jnp.bfloat16)
     up_grad = contract_rows(mlp_entry, hidden_grad)
     up_bias_grad = jnp.sum(hidden_grad.astype(jnp.float32), axis=0)
     mlp_entry_grad = contract_cols(hidden_grad, up_weight)
@@ -218,21 +538,13 @@
             jnp.sum(mlp_entry_grad, axis=0),
         ]
     )
-    grads_in = []
-    for first in range(0, count, chunk):
-        rows = slice(first, first + chunk)
-        entry = line_sum(both[rows], mp_size)
-        hat = xhat[rows]
-        inner = (
-            entry
-            - jnp.mean(entry, axis=-1, keepdims=True)
-            - hat * jnp.mean(entry * hat, axis=-1, keepdims=True)
-        )
-        grads_in.append(
-            (cotangent[rows].astype(jnp.float32) + factor[rows] * inner).astype(jnp.bfloat16)
-        )
-    input_grad = jnp.concatenate(grads_in)
-
+    entry = lax.psum(both, "mp")
+    inner = (
+        entry
+        - jnp.mean(entry, axis=-1, keepdims=True)
+        - xhat * jnp.mean(entry * xhat, axis=-1, keepdims=True)
+    )
+    input_grad = (cotangent.astype(jnp.float32) + factor * inner).astype(jnp.bfloat16)
     def scattered(array, dimension):
         return lax.psum_scatter(array, "dp", scatter_dimension=dimension, tiled=True)
 

time: 1230 us -> 1130 us (0.919)
  Pallas kernels: 0 us -> 222 us
  matrix products: 226 us -> 120 us
  starting transfers between devices: 96.2 us -> 0.25 us
  blocking collectives: 103 us -> 33.9 us
  other arithmetic: 104 us -> 47.1 us
  waiting for transfers between devices: 596 us -> 614 us
    ppermute x48 -> x0, waiting for transfers between devices: 596 us -> none  [the longest x16 368 us: line_sum(): came = lax.ppermute(total, 'mp', pairs)]
    reduce_scatter x4, waiting for transfers between devices: 0.01 us -> 323 us  [scattered(): lax.psum_scatter(array, 'dp', scatter_dimension=dimension, tiled=True)]
    psum x0 -> x1, waiting for transfers between devices: none -> 290 us  [per_device(): entry = lax.psum(both, 'mp')]
    pallas_call x0 -> x1, Pallas kernels: none -> 222 us  [layer_call(): pl.pallas_call(functools.partial(layer_kernel, size), out_shape=(jax.Shap...]
    ppermute x48 -> x0, starting transfers between devices: 95.9 us -> none  [the longest x16 59.2 us: line_sum(): total = total + lax.ppermute(total, 'mp', pairs)]
    dot_general x24 -> x0, matrix products: 74.3 us -> none  [the longest x8 37.2 us: per_device(): jnp.dot(mlp_entry[rows], up_weight, preferred_element_type=jnp.float32)]
    psum x1, blocking collectives: 81.1 us -> 9.45 us  [per_device(): norm_total = lax.psum(scattered(norm_grads, 1), 'mp')]
    add x25 -> x0, other arithmetic: 45.8 us -> none  [the longest x9 25.2 us: line_sum(): total = total + lax.ppermute(total, 'mp', pairs)]
  transfers between devices with their start and end apart: 53 -> 6, of which waited for: 25 -> 4; matrix products, arithmetic and copies ran while one was open for 14% -> 6% of each run, Pallas kernels for 0% -> 0%
where the time goes in v2:
time: 1130 us; the launch traced here: 1120 us
  waiting for transfers between devices  614 us (54%)
  Pallas kernels  222 us (20%)
  matrix products  120 us (11%)
  local copies, waits for them, and re-layouts  60 us (5%)
  other arithmetic  47.1 us (4%)
  blocking collectives  33.9 us (3%)
  between operations  16 us (1%)
    reduce_scatter x4, waiting for transfers between devices, scattered(): lax.psum_scatter(array, 'dp', scatter_dimension=dimension, tiled=True)  323 us
    psum x1, waiting for transfers between devices, per_device(): entry = lax.psum(both, 'mp')  290 us
    pallas_call x1, Pallas kernels, layer_call(): pl.pallas_call(functools.partial(layer_kernel, size), out_shape=(jax.Shap...  222 us
    dot_general x4, matrix products, contract_rows(): lax.dot_general(left, right, (((0,), (0,)), ((), ())), preferred_element_...  51.7 us
    dot_general x3, matrix products, contract_cols(): lax.dot_general(left, right, (((1,), (1,)), ((), ())), preferred_element_...  32.6 us
    unnamed x71, local copies, waits for them, and re-layouts  29 us
    unnamed x1, blocking collectives  24.4 us
  transfers between devices with their start and end apart: 6, of which 4 were waited for; matrix products, arithmetic and copies ran while one was open for 6% of the time, Pallas kernels for 0%

profile of v2, /device:TPU:0, one launch (start us, length us, event | category | flops | bytes accessed | tf_op | source)
XLA Modules:
  0.0 1119.6 jit_solution(306450917200613621)
XLA Ops:
  12.6 11.7 %convolution_add_fusion = f32[1024,1536]{1,0:T(8,128)} fusion(bf16[2048,1536]{1,0:T(8,128)(2,1)} %param.24, f32[1536]{0:T(1024)S(1)} %copy-done.30, bf16[1024,2048]{1,0:T(8,128)(2,1)S(1)} %copy-done, f32[2048]{0:T(1024)S(1)} %copy-done.31, f32[2048]{0:T(1024)S(1)} %copy-done.33, f32[1024]{0:T(1024)S(1)} %add_rsqrt_fusion, f32[1024]{0:T(1024)S(1)} %broadcast_multiply_fusion.3), kind=kOutput, calls=%fused_computation.76 | convolution fusion | flops 6456606720 | bytes 16807936 | tf_op jit(solution)/shard_map/dot_general | solution.py:429
  24.3 6.5 copy.73
  52.9 16.3 %while.28 = (s32[]{:T(128)}, bf16[2,512,2,256]{3,1,2,0:T(8,128)(2,1)}, f32[2,2,512]{2,1,0:T(2,128)S(1)}, s32[2]{0:T(128)S(1)}, s32[1024]{0:T(1024)S(1)}, /*index...) while((s32[]{:T(128)}, ...), condition=%wide.region_8.9_spmd.clone, body=%wide.region_5.8_spmd.clone.sunk | while | flops 1087897088 | bytes 26786052 | solution.py:464
  69.2 6.2 convolution_convert_fusion
  75.4 31.1 %while.29 = (s32[]{:T(128)}, f32[1024,2,256]{0,2,1:T(8,128)S(1)}, f32[1024,2,256]{0,2,1:T(8,128)}, f32[2,512,2,256]{3,1,0,2:T(8,128)}, s32[2]{0:T(128)S(1)}, /*i...) while((s32[]{:T(128)}, f32[1024,2,256]{0,2,1:T(8,128)S(1)}, ...), condition=%wide.region_11.12_spmd.clone, body=%wide.region_9.11_spmd.clone.sunk | while | flops 2704539136 | bytes 94415344 | solution.py:522
  108.7 3.5 split.32
  123.8 9.2 fusion.70
  133.0 3.2 fusion.48.mlp_entry
  136.2 221.6 %shard_map.237 = (bf16[1024,2048]{1,0:T(8,128)(2,1)}, bf16[1024,2048]{1,0:T(8,128)(2,1)}, bf16[1024,2048]{1,0:T(8,128)(2,1)}) custom-call(bf16[1024,2048]{1,0:T(8,128)(2,1)} %tokens.1, bf16[1024,2048]{1,0:T(8,128)(2,1)} %cotangent.1, bf16[1024,2048]{1,0:T(8,128)(2,1)} %fusion.48.mlp_entry, bf16[1024,512]{1,0:T(8,128)(2,1)} %bitcast.114, ...), custom_call_target="tpu_custom_call" | custom-call | flops 25769803776 | bytes 41943040 | tf_op jit(solution)/shard_map/pallas_call | solution.py:367
  357.8 17.2 %multiply_add_fusion = (f32[1024,2048]{1,0:T(8,128)}, f32[1024,2048]{1,0:T(8,128)}) fusion(f32[1024,2048]{1,0:T(8,128)} %fusion.70, f32[2048]{0:T(1024)S(1)} %copy-done.34, f32[2048]{0:T(1024)S(1)} %copy-done.28, bf16[1024,2048]{1,0:T(8,128)(2,1)} %get-tuple-element.134, bf16[2048,2048]{1,0:T(8,128)(2,1)} %up_weight.1), kind=kOutput, calls=%fused_computation.73 | convolution fusion | flops 8596226048 | bytes 37765120 | tf_op jit(solution)/shard_map/dot_general | solution.py:46
  375.0 290.3 %all-reduce.14.cloned.1.call-done = f32[1024,2048]{1,0:T(8,128)} async-done(((f32[1024,2048]{1,0:T(8,128)}), f32[1024,2048]{1,0:T(8,128)}) %all-reduce.14.cloned.1.call-update) | async-done | bytes 8388624 | tf_op jit(solution)/shard_map/psum | solution.py:541
  665.3 12.2 %fusion.66 = (f32[1024]{0:T(1024)S(1)}, f32[1024]{0:T(1024)S(1)}, f32[2048]{0:T(1024)S(1)}, f32[2048]{0:T(1024)S(1)}, f32[2048]{0:T(1024)S(1)}, /*index=5*/f32[2048]{0:T(1024)S(1)}) fusion(f32[1024,2048]{1,0:T(8,128)} %all-reduce.14.cloned.1.call-done, f32[1024]{0:T(1024)S(1)} %copy-done.26, f32[1024]{0:T(1024)S(1)} %copy-done.24, ...), kind=kLoop, calls=%fused_computation.119 | loop fusion | flops 25155584 | bytes 29409280 | tf_op jit(solution)/shard_map/reduce_sum | solution.py:544
  679.0 6.6 fusion.71
  687.6 14.1 %fusion.63 = f32[2048,1536]{1,0:T(8,128)} fusion(bf16[1024,1536]{0,1:T(8,128)(2,1)S(1)} %bitcast.121, bf16[1024,2048]{1,0:T(8,128)(2,1)} %tokens.1, f32[2048]{0:T(1024)S(1)} %copy-done.32, f32[2048]{0:T(1024)S(1)} %copy-done.34, f32[1024]{0:T(1024)S(1)} %copy-done.26, f32[1024]{0:T(1024)S(1)} %copy-done.24), kind=kOutput, calls=%fused_computation.118 | convolution fusion | flops 6455033856 | bytes 19947520 | tf_op jit(solution)/shard_map/dot_general | solution.py:40
  701.8 15.6 %fusion.72 = f32[2048,2048]{1,0:T(8,128)} fusion(bf16[1024,2048]{1,0:T(8,128)(2,1)} %fusion.48.mlp_entry, bf16[1024,2048]{1,0:T(8,128)(2,1)} %get-tuple-element.134), kind=kOutput, calls=%fused_computation.125 | convolution fusion | flops 8589934592 | bytes 25165824 | tf_op jit(solution)/shard_map/dot_general | solution.py:40
  717.4 15.4 %fusion.73 = f32[2048,2048]{1,0:T(8,128)} fusion(bf16[1024,2048]{1,0:T(8,128)(2,1)} %get-tuple-element.135, bf16[1024,2048]{1,0:T(8,128)(2,1)} %cotangent.1), kind=kOutput, calls=%fused_computation.126 | convolution fusion | flops 8589934592 | bytes 25165824 | tf_op jit(solution)/shard_map/dot_general | solution.py:40
  735.4 3.0 convert_reduce_fusion.2
  738.8 8.4 convert_reduce_fusion
  747.2 24.4 %all-reduce.11 = (f32[1536]{0:T(1024)S(1)}, f32[2048]{0:T(1024)S(1)}, f32[2048]{0:T(1024)S(1)}) all-reduce(f32[1536]{0:T(1024)S(1)} %reduce_sum.148, f32[2048]{0:T(1024)S(1)} %convert_reduce_fusion.2, f32[2048]{0:T(1024)S(1)} %get-tuple-element.329), channel_id=4, replica_groups=mesh['dp'=8,'mp'=4] {'dp'}, use_global_device_ids=true, to_apply=%region_23.24.clone | all-reduce | flops 5632 | bytes 45056
  774.6 9.4 psum.15
  784.6 82.4 %reduce-scatter.8.cloned.1.call-done = f32[256,1536]{1,0:T(8,128)} async-done(((f32[2048,1536]{1,0:T(8,128)}), f32[256,1536]{1,0:T(8,128)}) %reduce-scatter.8.cloned.1.call-update) | async-done | bytes 1572880 | tf_op jit(solution)/shard_map/reduce_scatter | solution.py:549
  867.0 120.4 %reduce-scatter.12.cloned.1.call-done = f32[256,2048]{1,0:T(8,128)} async-done(((f32[2048,2048]{1,0:T(8,128)}), f32[256,2048]{1,0:T(8,128)}) %reduce-scatter.12.cloned.1.call-update) | async-done | bytes 2097168 | tf_op jit(solution)/shard_map/reduce_scatter | solution.py:549
  987.4 120.4 %reduce-scatter.14.cloned.1.call-done = f32[2048,256]{1,0:T(8,128)} async-done(((f32[2048,2048]{1,0:T(8,128)}), f32[2048,256]{1,0:T(8,128)}) %reduce-scatter.14.cloned.1.call-update) | async-done | bytes 2097168 | tf_op jit(solution)/shard_map/reduce_scatter | solution.py:549
  1107.8 4.8 copy.144
  (201 shorter events, 90.0 us)
Async XLA Ops:
  7.2 658.2 %all-reduce.14.cloned.1.call-start = ((), (), s32[]{:S(2)}) async-start(), calls=%async_computation.5 | async-start | bytes 16777216 | tf_op jit(solution)/shard_map/psum | solution.py:541
  7.3 3.5 copy-start
  7.3 5.3 copy-start.30
  7.3 5.3 copy-start.31
  7.3 5.3 copy-start.33
  36.1 3.5 copy-start.6
  36.1 3.5 copy-start.29
  41.3 3.8 copy-start.14
  54.8 3.7 copy-start.20
  62.9 3.7 copy-start.20
  122.7 10.3 copy-start.12
  123.7 9.3 copy-start.1
  123.7 9.3 copy-start.24
  123.7 9.3 copy-start.26
  123.7 9.3 copy-start.27
  123.8 9.3 copy-start.28
  136.2 221.6 %copy-start.34 = (f32[2048]{0:T(1024)S(1)}, f32[2048]{0:T(1024)}, u32[]{:S(2)}) copy-start(f32[2048]{0:T(1024)} %param.20) | copy-start | bytes 24580
  374.9 398.6 %reduce-scatter.16.cloned.1.call-start = ((), (), s32[]{:S(2)}) async-start(), calls=%async_computation.10 | async-start | bytes 1179648
  665.3 13.7 %copy-start.8 = (bf16[128,8,2,256]{3,1,2,0:T(8,128)(2,1)S(1)}, bf16[128,8,2,256]{3,1,2,0:T(8,128)(2,1)}, u32[]{:S(2)}) copy-start(bf16[128,8,2,256]{3,1,2,0:T(8,128)(2,1)} %copy.117) | copy-start | bytes 3145732
  678.9 105.7 %reduce-scatter.10.cloned.1.call-start = ((), (), s32[]{:S(2)}) async-start(), calls=%async_computation.7 | async-start | bytes 4718592 | tf_op jit(solution)/shard_map/reduce_scatter | solution.py:549
  685.6 181.4 %reduce-scatter.8.cloned.1.call-start = ((), (), s32[]{:S(2)}) async-start(), calls=%async_computation.6 | async-start | bytes 14155776 | tf_op jit(solution)/shard_map/reduce_scatter | solution.py:549
  701.7 285.7 %reduce-scatter.12.cloned.1.call-start = ((), (), s32[]{:S(2)}) async-start(), calls=%async_computation.8 | async-start | bytes 18874368 | tf_op jit(solution)/shard_map/reduce_scatter | solution.py:549
  717.3 390.5 %reduce-scatter.14.cloned.1.call-start = ((), (), s32[]{:S(2)}) async-start(), calls=%async_computation.9 | async-start | bytes 18874368 | tf_op jit(solution)/shard_map/reduce_scatter | solution.py:549
  735.4 3.5 copy-start.2
  (29 other events, 52.6 us)
Sparse Core Ops, SparseCore 0:
  375.1 290.2 all-reduce.13
  679.1 35.0 reduce-scatter.15
  718.6 51.5 reduce-scatter.9
  774.6 92.3 reduce-scatter.7
  871.4 115.9 reduce-scatter.11
  991.8 115.9 reduce-scatter.13

commit v3 on v0

v3 whole, which is shorter than its diff:
```python
import functools
import math

import jax
import jax.numpy as jnp
from jax import lax
from jax.experimental import pallas as pl
from jax.experimental.pallas import tpu as pltpu
from jax.sharding import PartitionSpec as P

HEAD_DIM = 256
ROT = 64
EPSILON = 1e-05
LANES = 128

MESH = pl.DeviceIdType.MESH
ROWS = 64
SLOTS = 6
AHEAD = 2
CHUNK = 256
BLOCK = 32

F32 = jnp.float32
BF16 = jnp.bfloat16

VECTORS = 8
ATTN_GAIN, ATTN_SHIFT, MLP_GAIN, MLP_SHIFT, OUT_BIAS, UP_BIAS, QKV_BIAS = range(7)


def layout(lengths_row, count):
    ends = jnp.cumsum(lengths_row)
    places = jnp.arange(count, dtype=jnp.int32)
    passed = (places[:, None] >= ends[None, :]).astype(jnp.int32)
    return jnp.sum(passed * lengths_row[None, :], axis=1)


def rotary_tables(start, count):
    lane = jnp.arange(LANES, dtype=jnp.int32)[None, :]
    half = ROT // 2
    steps = (lane % half).astype(F32)
    freqs = jnp.exp(steps * (-2.0 * math.log(10000.0) / ROT))
    position = jnp.arange(count, dtype=jnp.int32) - start
    angle = position.astype(F32)[:, None] * freqs
    cosine = jnp.where(lane < ROT, jnp.cos(angle), 1.0)
    sine = jnp.sin(angle)
    sine = jnp.where(lane < half, -sine, jnp.where(lane < ROT, sine, 0.0))
    return cosine, sine


def normalize(rows):
    centred = rows - jnp.mean(rows, axis=-1, keepdims=True)
    factor = lax.rsqrt(jnp.mean(centred * centred, axis=-1, keepdims=True) + EPSILON)
    return centred * factor, factor


def gelu_parts(v):
    cdf = 0.5 + 0.5 * lax.erf(v * math.sqrt(0.5))
    return v * cdf, cdf + v * jnp.exp(-0.5 * v * v) * (1.0 / math.sqrt(2.0 * math.pi))


def dot(left, right):
    return jnp.dot(left, right, preferred_element_type=F32)


def dot_cols(left, right):
    return lax.dot_general(left, right, (((1,), (1,)), ((), ())), preferred_element_type=F32)


def dot_rows(left, right):
    return lax.dot_general(left, right, (((0,), (0,)), ((), ())), preferred_element_type=F32)


def column_sum(x):
    return jnp.sum(x, axis=0, keepdims=True)


def span(start, size):
    return pl.ds(pl.multiple_of(start, size), size)


class Spread:
    def __init__(self, bits, rows, cols):
        self.bits, self.rows, self.cols = bits, rows, cols
        self.tiles = 1 << bits
        self.orders = ([0] + list(range(1, bits)), [0] + list(range(bits - 1, 0, -1)))
        count = self.tiles // 2
        self.first = {}
        for stage in range(1, bits):
            for side in range(2):
                self.first[stage, side] = count
                count += self.tiles >> (stage + 1)
        self.sems = count

    def masks(self, side, stage):
        order = self.orders[side]
        return [m for m in range(self.tiles) if not any((m >> b) & 1 for b in order[:stage])]

    def place(self, mask, side, stage):
        return self.masks(side, stage + 1).index(mask)

    def shapes(self):
        shapes = [(self.tiles // 2, self.rows, self.cols)]
        for stage in range(self.bits):
            shapes.append((self.tiles >> (stage + 1), self.rows, self.cols))
        return shapes


def layer_kernel(mp_size, plans, *refs):
    refs = list(refs)

    def take(number):
        taken = refs[:number]
        del refs[:number]
        return taken

    tokens, cotangent, qkv_weight, dense_weight, up_weight, down_weight = take(6)
    attn_gain, attn_shift, mlp_gain, mlp_shift, qkv_bias, up_bias, out_bias = take(7)
    cosine, sine, start = take(3)
    layer_out, input_grad, vectors_out, parts = take(4)
    attn_entry, mlp_entry, attended, hidden, hidden_grad = take(5)
    spreads = [(plan, take(1 + plan.bits)) for plan in plans]
    from_outer, from_inner, sums, token_rows, cot_rows, out_rows = take(6)
    vectors, vectors_in, joined_grad = take(3)
    send_in, send_out, recv_outer, recv_inner, part_sems, row_sems, out_sems = take(7)
    vec_send, vec_recv = take(2)
    spread_sems = [take(2) for _ in plans]

    count, width = tokens.shape
    inner_width = up_weight.shape[1]
    heads_width = dense_weight.shape[0]
    local_heads = heads_width // HEAD_DIM
    bits = plans[0].bits
    steps = count // CHUNK
    scale = 1.0 / math.sqrt(HEAD_DIM)
    branch_messages = count // ROWS
    messages = 2 * branch_messages
    chunk_messages = CHUNK // ROWS
    half = mp_size // 2

    index = lax.axis_index("mp")
    upper = index // half
    level = index * (1 - upper) + (mp_size - 1 - index) * upper
    inner = index + 1 - 2 * upper
    outer = index - 1 + 2 * upper
    lag = half - level
    is_middle = level == half - 1
    device = lax.axis_index("dp")

    def partner(bit):
        return device + (1 - 2 * ((device // (1 << bit)) % 2)) * (1 << bit)

    def owner(mask):
        total = 0
        for bit in range(bits):
            total = total + ((device // (1 << bit) + mask // (1 << bit)) % 2) * (1 << bit)
        return total

    barrier = pltpu.get_barrier_semaphore()
    pl.semaphore_signal(barrier, inc=1, device_id={"mp": inner}, device_id_type=MESH)
    for bit in range(bits):
        pl.semaphore_signal(barrier, inc=1, device_id={"dp": partner(bit)}, device_id_type=MESH)
    if half > 1:

        @pl.when(level > 0)
        def _():
            pl.semaphore_signal(barrier, inc=1, device_id={"mp": outer}, device_id_type=MESH)
            pl.semaphore_wait(barrier, 2 + bits)

        @pl.when(level == 0)
        def _():
            pl.semaphore_wait(barrier, 1 + bits)

    else:
        pl.semaphore_wait(barrier, 1 + bits)


    def slot(ref, k):
        return ref.at[lax.rem(k, SLOTS)]

    def message(ref, k):
        return ref.at[span(k * ROWS, ROWS)]

    def to_inner(k, source, landing, sem):
        return pltpu.make_async_remote_copy(
            src_ref=source,
            dst_ref=slot(landing, k),
            send_sem=send_in.at[k],
            recv_sem=sem.at[k],
            device_id={"mp": inner},
            device_id_type=MESH,
        )

    def to_outer(k, source):
        return pltpu.make_async_remote_copy(
            src_ref=slot(source, k),
            dst_ref=slot(from_inner, k),
            send_sem=send_out.at[k],
            recv_sem=recv_inner.at[k],
            device_id={"mp": outer},
            device_id_type=MESH,
        )

    def load_part(k):
        return pltpu.make_async_copy(message(parts, k), slot(sums, k), part_sems.at[lax.rem(k, 2)])

    def load_rows(k):
        row, place = lax.rem(k, branch_messages), lax.rem(k, 2)
        return [
            pltpu.make_async_copy(
                message(tokens, row), token_rows.at[place], row_sems.at[0, place]
            ),
            pltpu.make_async_copy(
                message(cotangent, row), cot_rows.at[place], row_sems.at[1, place]
            ),
        ]

    def store_rows(k, target):
        place = lax.rem(k, 2)
        return pltpu.make_async_copy(
            out_rows.at[place], message(target, lax.rem(k, branch_messages)), out_sems.at[place]
        )

    def send_ahead(k):
        if half > 1:

            @pl.when((level == 0) & (k < messages))
            def _():
                to_inner(k, message(parts, k), from_outer, recv_outer).start()

    def begin_messages():
        for k in range(AHEAD):
            send_ahead(k)
        for copy in load_rows(0):
            copy.start()
        if half > 1:

            @pl.when(level > 0)
            def _():
                load_part(0).start()

        else:
            load_part(0).start()

    def add_inward(j):
        @pl.when(j < messages)
        def _():
            load_part(j).wait()

            @pl.when(j + 1 < messages)
            def _():
                load_part(j + 1).start()

            mine = slot(sums, j)
            if half > 1:
                to_inner(j, mine, from_outer, recv_outer).wait_recv()
                mine[...] += slot(from_outer, j)[...]

            @pl.when(is_middle)
            def _():
                to_inner(j, mine, from_inner, recv_inner).start()

            if half > 2:

                @pl.when(level < half - 1)
                def _():
                    to_inner(j, mine, from_outer, recv_outer).start()

    def finish(k, source):
        place = lax.rem(k, 2)

        @pl.when(k < branch_messages)
        def _():
            @pl.loop(0, ROWS // BLOCK)
            def _(b):
                rows = span(b * BLOCK, BLOCK)
                out_rows[place, rows] = (
                    token_rows[place, rows].astype(F32) + source[rows] + out_bias[...]
                ).astype(BF16)

        @pl.when(k >= branch_messages)
        def _():
            @pl.loop(0, ROWS // BLOCK)
            def _(b):
                rows = span(b * BLOCK, BLOCK)
                hat, factor = normalize(token_rows[place, rows].astype(F32))
                entry = source[rows]
                part = (
                    entry
                    - jnp.mean(entry, axis=-1, keepdims=True)
                    - hat * jnp.mean(entry * hat, axis=-1, keepdims=True)
                )
                out_rows[place, rows] = (
                    cot_rows[place, rows].astype(F32) + factor * part
                ).astype(BF16)

    def pass_outward(k):
        @pl.when((k >= 0) & (k < messages))
        def _():
            landed = slot(from_inner, k)
            total = slot(sums, k)
            to_outer(k, sums).wait_recv()
            to_inner(k, total, from_inner, recv_inner).wait_send()

            @pl.when(is_middle)
            def _():
                total[...] += landed[...]

            if half > 1:

                @pl.when(level > 0)
                def _():
                    @pl.when(k >= 1)
                    def _():
                        to_outer(k - 1, sums).wait_send()

                    @pl.when(is_middle)
                    def _():
                        to_outer(k, sums).start()

                    if half > 2:

                        @pl.when(level < half - 1)
                        def _():
                            to_outer(k, from_inner).start()

            @pl.when(k + 1 < messages)
            def _():
                for copy in load_rows(k + 1):
                    copy.start()

            for copy in load_rows(k):
                copy.wait()

            @pl.when(k >= 2)
            def _():
                store_rows(k - 2, layer_out).wait()

            @pl.when(is_middle)
            def _():
                finish(k, total)

            if half > 1:

                @pl.when(level < half - 1)
                def _():
                    finish(k, landed)

            @pl.when(k < branch_messages)
            def _():
                store_rows(k, layer_out).start()

            @pl.when(k >= branch_messages)
            def _():
                store_rows(k, input_grad).start()

    def service(j):
        send_ahead(j + AHEAD)
        if half > 1:

            @pl.when(level > 0)
            def _():
                add_inward(j)

        else:
            add_inward(j)
        pass_outward(j - lag)

    def end_messages():
        if half > 1:

            @pl.when(level > 0)
            def _():
                to_outer(messages - 1, sums).wait_send()

        for k in (messages - 2, messages - 1):
            store_rows(k, input_grad).wait()


    def spread_copy(number, stage, side, source, target, sem, bit):
        sends, recvs = spread_sems[number]
        return pltpu.make_async_remote_copy(
            src_ref=source,
            dst_ref=target,
            send_sem=sends.at[sem],
            recv_sem=recvs.at[sem],
            device_id={"dp": partner(bit)},
            device_id_type=MESH,
        )

    def side_rows(plan, side):
        return pl.ds(side * (plan.rows // 2), plan.rows // 2)

    def stage_copies(number, stage, side):
        plan, buffers = spreads[number]
        keep, landing = buffers[0], buffers[1 + stage]
        bit = plan.orders[side][stage]
        copies = []
        for mask in plan.masks(side, stage):
            if (mask >> bit) & 1:
                place = plan.place(mask ^ (1 << bit), side, stage)
                copies.append(
                    spread_copy(
                        number,
                        stage,
                        side,
                        keep.at[mask // 2, side_rows(plan, side)],
                        landing.at[place, side_rows(plan, side)],
                        plan.first[stage, side] + place,
                        bit,
                    )
                )
        return copies

    def tiles_out(number, compute, tile, sems):
        plan, buffers = spreads[number]
        half_tiles = plan.tiles // 2

        def copy(i):
            return spread_copy(
                number, 0, 0, tile.at[lax.rem(i, 2)], buffers[1].at[i], i, 0
            )

        @pl.loop(0, half_tiles)
        def _(i):
            @pl.when(i >= 2)
            def _():
                copy(i - 2).wait_send()

            compute(owner(2 * i + 1), tile.at[lax.rem(i, 2)])
            copy(i).start()

        for i in (half_tiles - 2, half_tiles - 1):
            copy(i).wait_send()

    def tiles_kept(number, compute, tile, landed, sems):
        plan, buffers = spreads[number]
        half_tiles = plan.tiles // 2

        def load(i):
            return pltpu.make_async_copy(buffers[1].at[i], landed, sems.at[0])

        def store(i):
            return pltpu.make_async_copy(
                tile.at[lax.rem(i, 2)], buffers[0].at[i], sems.at[1 + lax.rem(i, 2)]
            )

        @pl.loop(0, half_tiles)
        def _(i):
            spread_copy(
                number, 0, 0, tile.at[0], buffers[1].at[i], i, 0
            ).wait_recv()
            load(i).start()

            @pl.when(i >= 2)
            def _():
                store(i - 2).wait()

            compute(owner(2 * i), tile.at[lax.rem(i, 2)])
            load(i).wait()
            tile.at[lax.rem(i, 2)][...] += landed[...]
            store(i).start()

        for i in (half_tiles - 2, half_tiles - 1):
            store(i).wait()
        for side in range(2):
            for copy in stage_copies(number, 1, side):
                copy.start()

    def combine(number, stage, side):
        plan, buffers = spreads[number]
        keep, landing = buffers[0], buffers[1 + stage]
        rows = side_rows(plan, side)

        def run(mine, other, sems):
            for copy in stage_copies(number, stage, side):
                copy.wait_recv()
            for mask in plan.masks(side, stage + 1):
                place = plan.place(mask, side, stage)
                load_mine = pltpu.make_async_copy(keep.at[mask // 2, rows], mine, sems.at[0])
                load_other = pltpu.make_async_copy(landing.at[place, rows], other, sems.at[1])
                load_mine.start()
                load_other.start()
                load_mine.wait()
                load_other.wait()
                mine[...] += other[...]
                store = pltpu.make_async_copy(mine, keep.at[mask // 2, rows], sems.at[2])
                store.start()
                store.wait()
            for copy in stage_copies(number, stage + 1, side):
                copy.start()

        shape = (plan.rows // 2, plan.cols)
        pl.run_scoped(
            run, pltpu.VMEM(shape, F32), pltpu.VMEM(shape, F32), pltpu.SemaphoreType.DMA((3,))
        )

    def end_spread(number):
        plan, _ = spreads[number]
        for side in range(2):
            for copy in stage_copies(number, bits - 1, side):
                copy.wait_recv()
            for stage in range(1, bits):
                for copy in stage_copies(number, stage, side):
                    copy.wait_send()


    def vector_copy(place, device_id):
        return pltpu.make_async_remote_copy(
            src_ref=vectors,
            dst_ref=vectors_in.at[place],
            send_sem=vec_send.at[place],
            recv_sem=vec_recv.at[place],
            device_id=device_id,
            device_id_type=MESH,
        )

    def sum_vectors_dp(bit):
        copy = vector_copy(bit, {"dp": partner(bit)})
        copy.start()
        copy.wait()
        vectors[...] += vectors_in[bit]

    def sum_vectors_mp():
        norms = pl.ds(0, 4)
        for hop in range(half - 1):
            copy = vector_copy(bits, {"mp": inner})

            @pl.when(level == hop)
            def _():
                copy.start()
                copy.wait_send()

            @pl.when(level == hop + 1)
            def _():
                copy.wait_recv()
                vectors[norms] += vectors_in[bits, norms]

        across = vector_copy(bits + 1, {"mp": inner})

        @pl.when(is_middle)
        def _():
            across.start()
            across.wait()
            vectors[norms] += vectors_in[bits + 1, norms]

        for hop in reversed(range(half - 1)):
            copy = vector_copy(bits + 2, {"mp": outer})

            @pl.when(level == hop + 1)
            def _():
                copy.start()
                copy.wait_send()

            @pl.when(level == hop)
            def _():
                copy.wait_recv()
                vectors[norms] = vectors_in[bits + 2, norms]


    first_lanes = lax.broadcasted_iota(jnp.int32, (CHUNK, LANES), 1)

    def swap_halves(x):
        return jnp.where(
            first_lanes < ROT // 2,
            pltpu.roll(x, LANES - ROT // 2, 1),
            pltpu.roll(x, ROT // 2, 1),
        )

    def turn(x, rows, sign):
        low = x[:, :LANES]
        low = low * cosine[rows] + sign * swap_halves(low) * sine[rows]
        return jnp.concatenate([low, x[:, LANES:]], axis=1)

    def store_part(c, part, sem):
        copy = pltpu.make_async_copy(part, parts.at[span(c * CHUNK, CHUNK)], sem)
        copy.start()
        copy.wait()

    def forward(
        qkv,
        up,
        load_up,
        load_qkv,
        down,
        dense,
        keys,
        values,
        key_grad,
        value_grad,
        token_chunk,
        cot_chunk,
        attn_chunk,
        mlp_chunk,
        hidden_chunk,
        hidden_grad_chunk,
        part,
        probs,
        queries,
        attended_chunk,
        attended_grad,
        w_sems,
        in_sems,
        out_chunk_sems,
        part_sem,
    ):
        load_down = pltpu.make_async_copy(down_weight, down, w_sems.at[0])
        load_dense = pltpu.make_async_copy(dense_weight, dense, w_sems.at[1])
        tile = min(512, inner_width)
        wide = min(512, width)

        def load_tokens(c):
            return pltpu.make_async_copy(
                tokens.at[span(c * CHUNK, CHUNK)], token_chunk, in_sems.at[0]
            )

        def load_cot(c):
            return pltpu.make_async_copy(
                cotangent.at[span(c * CHUNK, CHUNK)],
                cot_chunk.at[lax.rem(c, 2)],
                in_sems.at[1 + lax.rem(c, 2)],
            )

        def chunk_stores(c):
            pairs = (
                (attn_chunk, attn_entry),
                (mlp_chunk, mlp_entry),
                (attended_chunk, attended),
                (hidden_chunk, hidden),
                (hidden_grad_chunk, hidden_grad),
            )
            return [
                pltpu.make_async_copy(
                    source, target.at[span(c * CHUNK, CHUNK)], out_chunk_sems.at[i]
                )
                for i, (source, target) in enumerate(pairs)
            ]

        load_tokens(0).start()
        load_qkv.start()
        load_up.start()
        load_dense.start()
        load_cot(0).start()
        load_down.start()
        keys[...] = jnp.zeros_like(keys)
        values[...] = jnp.zeros_like(values)
        key_grad[...] = jnp.zeros_like(key_grad)
        value_grad[...] = jnp.zeros_like(value_grad)
        vectors[...] = jnp.zeros_like(vectors)

        @pl.loop(0, steps)
        def _(c):
            rows = span(c * CHUNK, CHUNK)
            cot = cot_chunk.at[lax.rem(c, 2)]
            load_tokens(c).wait()

            @pl.when(c > 0)
            def _():
                for copy in chunk_stores(c - 1):
                    copy.wait()

            @pl.loop(0, CHUNK // BLOCK)
            def _(b):
                block = span(b * BLOCK, BLOCK)
                hat, _ = normalize(token_chunk[block].astype(F32))
                attn_chunk[block] = (hat * attn_gain[...] + attn_shift[...]).astype(BF16)
                mlp_chunk[block] = (hat * mlp_gain[...] + mlp_shift[...]).astype(BF16)

            @pl.when(c + 1 < steps)
            def _():
                load_tokens(c + 1).start()
                load_cot(c + 1).start()

            @pl.when(c == 0)
            def _():
                load_qkv.wait()

            for h in range(local_heads):
                cols = slice(h * HEAD_DIM, (h + 1) * HEAD_DIM)
                base = h * 3 * HEAD_DIM

                def joined(i):
                    there = slice(base + i * HEAD_DIM, base + (i + 1) * HEAD_DIM)
                    return dot(attn_chunk[...], qkv[:, there]) + qkv_bias[:, there]

                queries[:, cols] = turn(joined(0), rows, 1.0).astype(BF16)
                keys[rows, cols] = turn(joined(1), rows, 1.0).astype(BF16)
                values[rows, cols] = joined(2).astype(BF16)

            place = lax.broadcasted_iota(jnp.int32, (CHUNK, count), 1)
            here = lax.broadcasted_iota(jnp.int32, (CHUNK, count), 0) + c * CHUNK
            allowed = (place >= start[rows, :1]) & (place <= here)
            for h in range(local_heads):
                cols = slice(h * HEAD_DIM, (h + 1) * HEAD_DIM)
                scores = dot_cols(queries[:, cols], keys[:, cols]) * scale
                scores = jnp.where(allowed, scores, -1e30)
                expo = jnp.exp(scores - jnp.max(scores, axis=-1, keepdims=True))
                prob = expo * (1.0 / jnp.sum(expo, axis=-1, keepdims=True))
                probs[h] = prob
                attended_chunk[:, cols] = dot(prob.astype(BF16), values[:, cols]).astype(BF16)

            @pl.when(c == 0)
            def _():
                load_up.wait()
                load_down.wait()

            load_cot(c).wait()

            @pl.loop(0, inner_width // tile)
            def _(t):
                cols = span(t * tile, tile)
                pre = dot(mlp_chunk[...], up[:, cols]) + up_bias[:, cols]
                value, slope = gelu_parts(pre)
                hidden_chunk[:, cols] = value.astype(BF16)
                grad = (slope * dot_cols(cot[...], down[cols, :])).astype(BF16)
                hidden_grad_chunk[:, cols] = grad
                vectors[UP_BIAS : UP_BIAS + 1, cols] += column_sum(grad.astype(F32))

            @pl.when(c == 0)
            def _():
                load_dense.wait()

            @pl.loop(0, width // wide)
            def _(t):
                cols = span(t * wide, wide)
                part[:, cols] = dot(hidden_chunk[...], down[:, cols]) + dot(
                    attended_chunk[...], dense[:, cols]
                )

            store_part(c, part, part_sem.at[0])

            @pl.when(c == 0)
            def _():
                begin_messages()

            for copy in chunk_stores(c):
                copy.start()

            service(2 * c)

            attended_grad[...] = dot_cols(cot[...], dense[...]).astype(BF16)
            for h in range(local_heads):
                cols = slice(h * HEAD_DIM, (h + 1) * HEAD_DIM)
                base = h * 3 * HEAD_DIM
                grad = attended_grad[:, cols]
                prob = probs[h]
                prob_grad = dot_cols(grad, values[:, cols])
                along = jnp.sum(prob * prob_grad, axis=-1, keepdims=True)
                score_grad = (prob * (prob_grad - along)).astype(BF16)
                query_grad = dot(score_grad, keys[:, cols]) * scale
                joined_grad[rows, base : base + HEAD_DIM] = turn(query_grad, rows, -1.0).astype(
                    BF16
                )
                key_grad[:, cols] += dot_rows(score_grad, queries[:, cols]) * scale
                value_grad[:, cols] += dot_rows(prob.astype(BF16), grad)

            @pl.loop(0, CHUNK // BLOCK)
            def _(b):
                block = span(b * BLOCK, BLOCK)
                vectors[OUT_BIAS : OUT_BIAS + 1, :width] += column_sum(cot[block].astype(F32))

            service(2 * c + 1)

        for copy in chunk_stores(steps - 1):
            copy.wait()

        @pl.loop(0, steps)
        def _(c):
            rows = span(c * CHUNK, CHUNK)
            for h in range(local_heads):
                cols = slice(h * HEAD_DIM, (h + 1) * HEAD_DIM)
                base = h * 3 * HEAD_DIM
                joined_grad[rows, base + HEAD_DIM : base + 2 * HEAD_DIM] = turn(
                    key_grad[rows, cols], rows, -1.0
                ).astype(BF16)
                joined_grad[rows, base + 2 * HEAD_DIM : base + 3 * HEAD_DIM] = value_grad[
                    rows, cols
                ].astype(BF16)

    def backward(qkv, up, grad_chunk, token_chunk, hat, part, in_sems, part_sem, first_slot):
        wide = min(512, width)

        def loads(c):
            rows = span(c * CHUNK, CHUNK)
            return [
                pltpu.make_async_copy(
                    hidden_grad.at[rows], grad_chunk.at[lax.rem(c, 2)], in_sems.at[lax.rem(c, 2), 0]
                ),
                pltpu.make_async_copy(
                    tokens.at[rows], token_chunk.at[lax.rem(c, 2)], in_sems.at[lax.rem(c, 2), 1]
                ),
            ]

        for copy in loads(0):
            copy.start()

        @pl.loop(0, steps)
        def _(c):
            rows = span(c * CHUNK, CHUNK)
            for copy in loads(c):
                copy.wait()

            @pl.when(c + 1 < steps)
            def _():
                for copy in loads(c + 1):
                    copy.start()

            @pl.loop(0, CHUNK // BLOCK)
            def _(b):
                block = span(b * BLOCK, BLOCK)
                hat[block] = normalize(token_chunk[lax.rem(c, 2), block].astype(F32))[0]

            vectors[QKV_BIAS : QKV_BIAS + 1, : 3 * heads_width] += column_sum(
                joined_grad[rows].astype(F32)
            )

            @pl.loop(0, width // wide)
            def _(t):
                cols = span(t * wide, wide)
                attn_grad = dot_cols(joined_grad[rows], qkv[cols, :])
                mlp_grad = dot_cols(grad_chunk[lax.rem(c, 2)], up[cols, :])
                part[:, cols] = attn_grad * attn_gain[:, cols] + mlp_grad * mlp_gain[:, cols]
                near = hat[:, cols]
                for row, value in (
                    (ATTN_GAIN, attn_grad * near),
                    (ATTN_SHIFT, attn_grad),
                    (MLP_GAIN, mlp_grad * near),
                    (MLP_SHIFT, mlp_grad),
                ):
                    vectors[row : row + 1, cols] += column_sum(value)

            store_part(steps + c, part, part_sem.at[0])
            service(first_slot + c)

    def fill(source, target, sem):
        return pltpu.make_async_copy(source, target, sem)

    def spread_columns(number, left_source, first_slot, split):
        plan, _ = spreads[number]
        depth = left_source.shape[1]

        def run(left, turned, right, tile, landed, sems):
            loads = [fill(left_source, left, sems.at[0]), fill(cotangent, right, sems.at[1])]
            for copy in loads:
                copy.start()
            for copy in loads:
                copy.wait()

            @pl.loop(0, depth // HEAD_DIM)
            def _(b):
                there = span(b * HEAD_DIM, HEAD_DIM)
                turned[there, :] = left[:, there].T

            def compute(where, target):
                right_cols = right[:, span(where * plan.cols, plan.cols)]
                block = min(512, depth)

                @pl.loop(0, depth // block)
                def _(b):
                    there = span(b * block, block)
                    target[there, :] = dot(turned[there, :], right_cols)

            tiles_out(number, compute, tile, sems)
            if split:
                service(first_slot)
            tiles_kept(number, compute, tile, landed, sems)
            service(first_slot + split)

        pl.run_scoped(
            run,
            pltpu.VMEM((count, depth), BF16),
            pltpu.VMEM((depth, count), BF16),
            pltpu.VMEM((count, width), BF16),
            pltpu.VMEM((2, plan.rows, plan.cols), F32),
            pltpu.VMEM((plan.rows, plan.cols), F32),
            pltpu.SemaphoreType.DMA((3,)),
        )

    def spread_rows(number, left_source, right_source, first_slot, split):
        plan, _ = spreads[number]

        def run(left, right, tile, landed, sems):
            loads = [fill(left_source, left, sems.at[0])]
            if right_source is not joined_grad:
                loads.append(fill(right_source, right, sems.at[1]))
            for copy in loads:
                copy.start()
            for copy in loads:
                copy.wait()
            use = joined_grad if right_source is joined_grad else right

            def compute(where, target):
                turned = left[:, span(where * plan.rows, plan.rows)].T
                block = min(512, plan.cols)

                @pl.loop(0, plan.cols // block)
                def _(b):
                    there = span(b * block, block)
                    target[:, there] = dot(turned, use[:, there])

            tiles_out(number, compute, tile, sems)
            if split:
                service(first_slot)
            tiles_kept(number, compute, tile, landed, sems)
            service(first_slot + split)

        right_shape = (16, LANES) if right_source is joined_grad else (count, plan.cols)
        pl.run_scoped(
            run,
            pltpu.VMEM((count, width), BF16),
            pltpu.VMEM(right_shape, BF16),
            pltpu.VMEM((2, plan.rows, plan.cols), F32),
            pltpu.VMEM((plan.rows, plan.cols), F32),
            pltpu.SemaphoreType.DMA((3,)),
        )

    QKV, DENSE, UP, DOWN = range(4)
    slots = [2 * steps]

    def take_slots(number):
        slots[0] += number
        return slots[0] - number

    def with_weights(qkv, up, w_sems):
        load_qkv = pltpu.make_async_copy(qkv_weight, qkv, w_sems.at[0])
        load_up = pltpu.make_async_copy(up_weight, up, w_sems.at[1])
        pl.run_scoped(
            functools.partial(forward, qkv, up, load_up, load_qkv),
            pltpu.VMEM(down_weight.shape, BF16),
            pltpu.VMEM(dense_weight.shape, BF16),
            pltpu.VMEM((count, heads_width), BF16),
            pltpu.VMEM((count, heads_width), BF16),
            pltpu.VMEM((count, heads_width), F32),
            pltpu.VMEM((count, heads_width), F32),
            pltpu.VMEM((CHUNK, width), BF16),
            pltpu.VMEM((2, CHUNK, width), BF16),
            pltpu.VMEM((CHUNK, width), BF16),
            pltpu.VMEM((CHUNK, width), BF16),
            pltpu.VMEM((CHUNK, inner_width), BF16),
            pltpu.VMEM((CHUNK, inner_width), BF16),
            pltpu.VMEM((CHUNK, width), F32),
            pltpu.VMEM((local_heads, CHUNK, count), F32),
            pltpu.VMEM((CHUNK, heads_width), BF16),
            pltpu.VMEM((CHUNK, heads_width), BF16),
            pltpu.VMEM((CHUNK, heads_width), BF16),
            pltpu.SemaphoreType.DMA((2,)),
            pltpu.SemaphoreType.DMA((3,)),
            pltpu.SemaphoreType.DMA((5,)),
            pltpu.SemaphoreType.DMA((1,)),
        )
        spread_columns(DOWN, hidden, take_slots(2), 1)
        spread_columns(DENSE, attended, take_slots(1), 0)
        first = take_slots(steps)
        pl.run_scoped(
            lambda *scratch: backward(qkv, up, *scratch, first),
            pltpu.VMEM((2, CHUNK, inner_width), BF16),
            pltpu.VMEM((2, CHUNK, width), BF16),
            pltpu.VMEM((CHUNK, width), F32),
            pltpu.VMEM((CHUNK, width), F32),
            pltpu.SemaphoreType.DMA((2, 2)),
            pltpu.SemaphoreType.DMA((1,)),
        )

    pl.run_scoped(
        with_weights,
        pltpu.VMEM(qkv_weight.shape, BF16),
        pltpu.VMEM(up_weight.shape, BF16),
        pltpu.SemaphoreType.DMA((2,)),
    )
    spread_rows(UP, mlp_entry, hidden_grad, take_slots(2), 1)
    spread_rows(QKV, attn_entry, joined_grad, take_slots(2), 1)
    for stage in range(1, bits - 1):
        for number in (DOWN, DENSE, UP, QKV):
            for side in range(2):
                combine(number, stage, side)
                if number != DENSE or side:
                    service(take_slots(1))
    for bit in range(bits):
        sum_vectors_dp(bit)
    service(take_slots(1))
    sum_vectors_mp()

    @pl.loop(slots[0], messages + half)
    def _(j):
        service(j)

    end_messages()
    for number in (DOWN, DENSE, UP, QKV):
        end_spread(number)
    store_vectors = fill(vectors, vectors_out, vec_send.at[0])
    store_vectors.start()
    store_vectors.wait()


def layer_call(mp_size, dp_size, operands):
    tokens, qkv, dense, up, down = (operands[i] for i in (0, 2, 3, 4, 5))
    count, width = tokens.shape
    inner_width, heads_width = up.shape[1], dense.shape[0]
    messages = 2 * (count // ROWS)
    bits = dp_size.bit_length() - 1
    owned = width // dp_size
    plans = (
        Spread(bits, owned, qkv.shape[1]),
        Spread(bits, heads_width, owned),
        Spread(bits, owned, inner_width),
        Spread(bits, inner_width, owned),
    )
    vector_width = max(width, inner_width, qkv.shape[1])
    anywhere = pl.BlockSpec(memory_space=pl.ANY)
    vmem = pl.BlockSpec(memory_space=pltpu.VMEM)
    shape = jax.ShapeDtypeStruct
    out_shape = [
        shape((count, width), BF16),
        shape((count, width), BF16),
        shape((VECTORS, vector_width), F32),
        shape((2 * count, width), F32),
        shape((count, width), BF16),
        shape((count, width), BF16),
        shape((count, heads_width), BF16),
        shape((count, inner_width), BF16),
        shape((count, inner_width), BF16),
    ]
    for plan in plans:
        out_shape += [shape(dims, F32) for dims in plan.shapes()]
    dma = pltpu.SemaphoreType.DMA
    scratch = [
        pltpu.VMEM((SLOTS, ROWS, width), F32),
        pltpu.VMEM((SLOTS, ROWS, width), F32),
        pltpu.VMEM((SLOTS, ROWS, width), F32),
        pltpu.VMEM((2, ROWS, width), BF16),
        pltpu.VMEM((2, ROWS, width), BF16),
        pltpu.VMEM((2, ROWS, width), BF16),
        pltpu.VMEM((VECTORS, vector_width), F32),
        pltpu.VMEM((bits + 3, VECTORS, vector_width), F32),
        pltpu.VMEM((count, qkv.shape[1]), BF16),
        dma((messages,)),
        dma((messages,)),
        dma((messages,)),
        dma((messages,)),
        dma((2,)),
        dma((2, 2)),
        dma((2,)),
        dma((bits + 3,)),
        dma((bits + 3,)),
    ]
    for plan in plans:
        scratch += [dma((plan.sems,)), dma((plan.sems,))]
    results = pl.pallas_call(
        functools.partial(layer_kernel, mp_size, plans),
        out_shape=tuple(out_shape),
        in_specs=[anywhere] * 6 + [vmem] * 10,
        out_specs=(anywhere,) * len(out_shape),
        scratch_shapes=scratch,
        compiler_params=pltpu.CompilerParams(
            collective_id=0, has_side_effects=True, vmem_limit_bytes=62 * 1024 * 1024
        ),
        cost_estimate=pl.CostEstimate(
            flops=6 * count * (width * (qkv.shape[1] + 2 * inner_width + heads_width)),
            bytes_accessed=300 << 20,
            transcendentals=0,
        ),
    )(*operands)
    layer_output, input_grad, vectors = results[:3]
    spread = list(results[9:])
    grads = []
    for plan in plans:
        buffers, spread = spread[: 1 + bits], spread[1 + bits :]
        grads.append(buffers[0][0] + buffers[bits][0])
    return layer_output, input_grad, vectors, grads


def per_device(
    mp_size,
    dp_size,
    tokens,
    lengths,
    attn_gain,
    attn_shift,
    mlp_gain,
    mlp_shift,
    qkv_weight,
    qkv_bias,
    dense_weight,
    up_weight,
    up_bias,
    down_weight,
    out_bias,
    cotangent,
):
    count, width = tokens.shape
    start = layout(lengths[0], count)
    cosine, sine = rotary_tables(start, count)
    start = jnp.broadcast_to(start[:, None], (count, LANES))
    layer_output, input_grad, vectors, grads = layer_call(
        mp_size,
        dp_size,
        (
            tokens,
            cotangent,
            qkv_weight,
            dense_weight,
            up_weight,
            down_weight,
            attn_gain[None],
            attn_shift[None],
            mlp_gain[None],
            mlp_shift[None],
            qkv_bias[None],
            up_bias[None],
            out_bias[None],
            cosine,
            sine,
            start,
        ),
    )
    qkv_grad, dense_grad, up_grad, down_grad = grads
    me = lax.axis_index("dp")

    def owned(row, total):
        return lax.dynamic_slice_in_dim(vectors[row], me * (total // dp_size), total // dp_size)

    return (
        layer_output,
        input_grad,
        owned(ATTN_GAIN, width),
        owned(ATTN_SHIFT, width),
        owned(MLP_GAIN, width),
        owned(MLP_SHIFT, width),
        qkv_grad,
        owned(QKV_BIAS, qkv_weight.shape[1]),
        dense_grad,
        up_grad,
        owned(UP_BIAS, up_weight.shape[1]),
        down_grad,
        owned(OUT_BIAS, width),
    )


def solution(mesh):
    in_specs = (
        P("dp", None),
        P("dp", None),
        P(),
        P(),
        P(),
        P(),
        P(None, "mp"),
        P("mp"),
        P("mp", None),
        P(None, "mp"),
        P("mp"),
        P("mp", None),
        P(),
        P("dp", None),
    )
    out_specs = (
        P("dp", None),
        P("dp", None),
        P("dp"),
        P("dp"),
        P("dp"),
        P("dp"),
        P("dp", "mp"),
        P(("mp", "dp")),
        P("mp", "dp"),
        P("dp", "mp"),
        P(("mp", "dp")),
        P("mp", "dp"),
        P("dp"),
    )
    function = functools.partial(per_device, mesh.shape["mp"], mesh.shape["dp"])
    return jax.shard_map(
        function, mesh=mesh, in_specs=in_specs, out_specs=out_specs, check_vma=False
    )
```

time: 1140 us -> 523 us (0.46)
  waiting for transfers between devices: 781 us -> 0 us
  Pallas kernels: 0 us -> 489 us
  matrix products: 182 us -> 0 us
  other arithmetic: 63.1 us -> 16.5 us
  local copies, waits for them, and re-layouts: 57.4 us -> 14.5 us
  blocking collectives: 24.6 us -> 0 us
  between operations: 18.2 us -> 0.7 us
    psum x1 -> x0, waiting for transfers between devices: 781 us -> none  [per_device(): branch = lax.psum(partial_sum, 'mp')]
    pallas_call x0 -> x1, Pallas kernels: none -> 489 us  [layer_call(): pl.pallas_call(functools.partial(layer_kernel, mp_size, plans), out_shape...]
    dot_general x26 -> x0, matrix products: 182 us -> none  [the longest x4 58.3 us: contract_cols(): lax.dot_general(left, right, (((1,), (1,)), ((), ())), preferred_element_...]
    reduce_sum x9 -> x1, other arithmetic: 38.7 us -> 0.74 us  [layout(): return jnp.sum(passed * lengths_row[None, :], axis=1)]
    unnamed x1 -> x0, blocking collectives: 24.6 us -> none
    unnamed x104 -> x10, local copies, waits for them, and re-layouts: 24.5 us -> 6.97 us
    add x4, other arithmetic: 0.01 us -> 11.8 us  [layer_call(): grads.append(buffers[0][0] + buffers[bits][0])]
  transfers between devices with their start and end apart: 5 -> 0, of which waited for: 1 -> 0; matrix products, arithmetic and copies ran while one was open for 8% -> 0% of each run, Pallas kernels for 0% -> 0%
where the time goes in v3:
time: 523 us; the launch traced here: 521 us
  Pallas kernels  489 us (93%)
  other arithmetic  16.5 us (3%)
  local copies, waits for them, and re-layouts  14.5 us (3%)
    pallas_call x1, Pallas kernels, layer_call(): pl.pallas_call(functools.partial(layer_kernel, mp_size, plans), out_shape...  489 us
    add x4, other arithmetic, layer_call(): grads.append(buffers[0][0] + buffers[bits][0])  11.8 us

profile of v3, /device:TPU:0, one launch (start us, length us, event | category | flops | bytes accessed | tf_op | source)
XLA Modules:
  0.0 521.1 jit_solution(4276515521708939153)
XLA Ops:
  0.6 0.8 reduce-window.8
  1.5 0.7 select_reduce_fusion
  2.3 3.1 fusion.2
  5.4 1.0 broadcast_in_dim.70.refs_15_
  6.4 1.3 broadcast_in_dim.63.refs_10_
  7.7 489.5 %shard_map.237 = (bf16[1024,2048]{1,0:T(8,128)(2,1)}, bf16[1024,2048]{1,0:T(8,128)(2,1)}, f32[8,2048]{1,0:T(8,128)}, f32[2048,2048]{1,0:T(8,128)}, bf16[1024,204...) custom-call(bf16[1024,2048]{1,0:T(8,128)(2,1)} %refs_0_.1, ...), custom_call_target="tpu_custom_call" | custom-call | flops 77309411328 | bytes 314572800 | tf_op jit(solution)/shard_map/pallas_call | solution.py:1047
  497.1 0.0 copy-start.1
  497.1 1.2 fusion.7
  498.4 0.6 constant_dynamic-slice_fusion.4
  498.9 0.6 constant_dynamic-slice_fusion.3
  499.5 0.6 constant_dynamic-slice_fusion.2
  500.1 0.6 constant_dynamic-slice_fusion
  500.6 0.6 constant_dynamic-slice_fusion.6
  501.2 0.6 constant_dynamic-slice_fusion.5
  501.7 3.8 add_bitcast_fusion
  505.6 0.0 copy-done.1
  505.6 3.3 add_bitcast_fusion.1
  508.9 0.0 copy-done.3
  508.9 1.9 add_bitcast_fusion.3
  510.8 0.0 copy-done.2
  510.8 2.8 add_bitcast_fusion.2
  513.5 0.6 constant_dynamic-slice_fusion.1
  514.2 4.9 copy.29
  519.1 2.0 copy.30
  (7 shorter events, 0.0 us)
Async XLA Ops:
  497.1 8.4 %copy-start.1 = (f32[1,256,2048]{2,1,0:T(8,128)S(1)}, f32[1,256,2048]{2,1,0:T(8,128)}, u32[]{:S(2)}) copy-start(f32[1,256,2048]{2,1,0:T(8,128)} %get-tuple-element.32) | copy-start | bytes 6291460
  505.6 3.3 copy-start.3
  505.6 5.2 %copy-start.2 = (f32[1,256,1536]{2,1,0:T(8,128)S(1)}, f32[1,256,1536]{2,1,0:T(8,128)}, u32[]{:S(2)}) copy-start(f32[1,256,1536]{2,1,0:T(8,128)} %get-tuple-element.28) | copy-start | bytes 4718596
  514.2 4.9 copy-start

commit v4 on v3

--- a/solution.py
+++ b/solution.py
@@ -27,22 +27,39 @@
 ATTN_GAIN, ATTN_SHIFT, MLP_GAIN, MLP_SHIFT, OUT_BIAS, UP_BIAS, QKV_BIAS = range(7)
 
 
-def layout(lengths_row, count):
-    ends = jnp.cumsum(lengths_row)
-    places = jnp.arange(count, dtype=jnp.int32)
-    passed = (places[:, None] >= ends[None, :]).astype(jnp.int32)
-    return jnp.sum(passed * lengths_row[None, :], axis=1)
-
-
-def rotary_tables(start, count):
-    lane = jnp.arange(LANES, dtype=jnp.int32)[None, :]
+def sine_cosine(angle):
+    turns = jnp.floor(angle * (2.0 / math.pi) + 0.5)
+    rest = angle - turns * 1.5703125 - turns * 4.837512969970703e-4 - turns * 7.549789954891882e-8
+    square = rest * rest
+    sine = rest + rest * square * (
+        -1.6666654611e-1 + square * (8.3321608736e-3 - square * 1.9515295891e-4)
+    )
+    cosine = (
+        1.0
+        - 0.5 * square
+        + square
+        * square
+        * (4.166664568298827e-2 + square * (-1.388731625493765e-3 + square * 2.443315711809948e-5))
+    )
+    quarter = turns - 4.0 * jnp.floor(turns * 0.25)
+    odd = (quarter == 1.0) | (quarter == 3.0)
+    flip_sine = quarter >= 2.0
+    flip_cosine = (quarter == 1.0) | (quarter == 2.0)
+    near_sine = jnp.where(odd, cosine, sine)
+    near_cosine = jnp.where(odd, sine, cosine)
+    return (
+        jnp.where(flip_sine, -near_sine, near_sine),
+        jnp.where(flip_cosine, -near_cosine, near_cosine),
+    )
+
+
+def rotary_tables(place, start):
+    lane = lax.broadcasted_iota(jnp.int32, place.shape, 1)
     half = ROT // 2
-    steps = (lane % half).astype(F32)
-    freqs = jnp.exp(steps * (-2.0 * math.log(10000.0) / ROT))
-    position = jnp.arange(count, dtype=jnp.int32) - start
-    angle = position.astype(F32)[:, None] * freqs
-    cosine = jnp.where(lane < ROT, jnp.cos(angle), 1.0)
-    sine = jnp.sin(angle)
+    step = jnp.where(lane < half, lane, lane - half).astype(F32)
+    freqs = jnp.exp(step * (-2.0 * math.log(10000.0) / ROT))
+    sine, cosine = sine_cosine((place - start).astype(F32) * freqs)
+    cosine = jnp.where(lane < ROT, cosine, 1.0)
     sine = jnp.where(lane < half, -sine, jnp.where(lane < ROT, sine, 0.0))
     return cosine, sine
 
@@ -115,12 +132,13 @@
 
     tokens, cotangent, qkv_weight, dense_weight, up_weight, down_weight = take(6)
     attn_gain, attn_shift, mlp_gain, mlp_shift, qkv_bias, up_bias, out_bias = take(7)
-    cosine, sine, start = take(3)
+    lengths = take(1)[0]
     layer_out, input_grad, vectors_out, parts = take(4)
+    grads_out = take(len(plans))
     attn_entry, mlp_entry, attended, hidden, hidden_grad = take(5)
     spreads = [(plan, take(1 + plan.bits)) for plan in plans]
     from_outer, from_inner, sums, token_rows, cot_rows, out_rows = take(6)
-    vectors, vectors_in, joined_grad = take(3)
+    vectors, vectors_in, joined_grad, cosine, sine = take(5)
     send_in, send_out, recv_outer, recv_inner, part_sems, row_sems, out_sems = take(7)
     vec_send, vec_recv = take(2)
     spread_sems = [take(2) for _ in plans]
@@ -143,6 +161,7 @@
     inner = index + 1 - 2 * upper
     outer = index - 1 + 2 * upper
     lag = half - level
+    ahead = min(AHEAD, SLOTS - 1 - half)
     is_middle = level == half - 1
     device = lax.axis_index("dp")
 
@@ -228,7 +247,7 @@
                 to_inner(k, message(parts, k), from_outer, recv_outer).start()
 
     def begin_messages():
-        for k in range(AHEAD):
+        for k in range(ahead):
             send_ahead(k)
         for copy in load_rows(0):
             copy.start()
@@ -354,7 +373,7 @@
                 store_rows(k, input_grad).start()
 
     def service(j):
-        send_ahead(j + AHEAD)
+        send_ahead(j + ahead)
         if half > 1:
 
             @pl.when(level > 0)
@@ -469,36 +488,55 @@
     def combine(number, stage, side):
         plan, buffers = spreads[number]
         keep, landing = buffers[0], buffers[1 + stage]
-        rows = side_rows(plan, side)
+        last = stage == bits - 1
+        rows = plan.rows // 4
 
         def run(mine, other, sems):
             for copy in stage_copies(number, stage, side):
                 copy.wait_recv()
+            loads, stores = [], []
             for mask in plan.masks(side, stage + 1):
                 place = plan.place(mask, side, stage)
-                load_mine = pltpu.make_async_copy(keep.at[mask // 2, rows], mine, sems.at[0])
-                load_other = pltpu.make_async_copy(landing.at[place, rows], other, sems.at[1])
-                load_mine.start()
-                load_other.start()
-                load_mine.wait()
-                load_other.wait()
-                mine[...] += other[...]
-                store = pltpu.make_async_copy(mine, keep.at[mask // 2, rows], sems.at[2])
+                for piece in range(2):
+                    there = pl.ds(side * (plan.rows // 2) + piece * rows, rows)
+                    at = len(loads) % 2
+                    kept = keep.at[mask // 2, there]
+                    loads.append(
+                        [
+                            pltpu.make_async_copy(kept, mine.at[at], sems.at[0, at]),
+                            pltpu.make_async_copy(
+                                landing.at[place, there], other.at[at], sems.at[1, at]
+                            ),
+                        ]
+                    )
+                    target = grads_out[number].at[there] if last else kept
+                    stores.append(pltpu.make_async_copy(mine.at[at], target, sems.at[2, at]))
+            for copy in loads[0]:
+                copy.start()
+            for i, (load, store) in enumerate(zip(loads, stores)):
+                if i + 1 < len(loads):
+                    if i >= 1:
+                        stores[i - 1].wait()
+                    for copy in loads[i + 1]:
+                        copy.start()
+                for copy in load:
+                    copy.wait()
+                mine[i % 2] += other[i % 2]
                 store.start()
+            for store in stores[-2:]:
                 store.wait()
-            for copy in stage_copies(number, stage + 1, side):
-                copy.start()
-
-        shape = (plan.rows // 2, plan.cols)
+            if not last:
+                for copy in stage_copies(number, stage + 1, side):
+                    copy.start()
+
+        shape = (2, rows, plan.cols)
         pl.run_scoped(
-            run, pltpu.VMEM(shape, F32), pltpu.VMEM(shape, F32), pltpu.SemaphoreType.DMA((3,))
+            run, pltpu.VMEM(shape, F32), pltpu.VMEM(shape, F32), pltpu.SemaphoreType.DMA((3, 2))
         )
 
     def end_spread(number):
         plan, _ = spreads[number]
         for side in range(2):
-            for copy in stage_copies(number, bits - 1, side):
-                copy.wait_recv()
             for stage in range(1, bits):
                 for copy in stage_copies(number, stage, side):
                     copy.wait_send()
@@ -514,47 +552,83 @@
             device_id_type=MESH,
         )
 
-    def sum_vectors_dp(bit):
-        copy = vector_copy(bit, {"dp": partner(bit)})
-        copy.start()
-        copy.wait()
-        vectors[...] += vectors_in[bit]
-
-    def sum_vectors_mp():
-        norms = pl.ds(0, 4)
-        for hop in range(half - 1):
-            copy = vector_copy(bits, {"mp": inner})
-
+    norms = pl.ds(0, 4)
+
+    def inward_hop(hop):
+        return vector_copy(bits + hop, {"mp": inner})
+
+    def outward_hop(hop):
+        return vector_copy(bits + half + hop, {"mp": outer})
+
+    def vector_steps():
+        steps = []
+
+        def start_inward(hop):
             @pl.when(level == hop)
             def _():
-                copy.start()
-                copy.wait_send()
-
+                inward_hop(hop).start()
+
+        def end_inward(hop):
+            @pl.when(level == hop)
+            def _():
+                inward_hop(hop).wait_send()
+
+            if hop < half - 1:
+
+                @pl.when(level == hop + 1)
+                def _():
+                    inward_hop(hop).wait_recv()
+                    vectors[norms] += vectors_in[bits + hop, norms]
+
+            else:
+
+                @pl.when(is_middle)
+                def _():
+                    inward_hop(hop).wait_recv()
+                    vectors[norms] += vectors_in[bits + hop, norms]
+
+        def start_outward(hop):
             @pl.when(level == hop + 1)
             def _():
-                copy.wait_recv()
-                vectors[norms] += vectors_in[bits, norms]
-
-        across = vector_copy(bits + 1, {"mp": inner})
-
-        @pl.when(is_middle)
-        def _():
-            across.start()
-            across.wait()
-            vectors[norms] += vectors_in[bits + 1, norms]
-
-        for hop in reversed(range(half - 1)):
-            copy = vector_copy(bits + 2, {"mp": outer})
-
+                outward_hop(hop).start()
+
+        def end_outward(hop):
             @pl.when(level == hop + 1)
             def _():
-                copy.start()
-                copy.wait_send()
+                outward_hop(hop).wait_send()
 
             @pl.when(level == hop)
             def _():
-                copy.wait_recv()
-                vectors[norms] = vectors_in[bits + 2, norms]
+                outward_hop(hop).wait_recv()
+                vectors[norms] = vectors_in[bits + half + hop, norms]
+
+        def start_across(bit):
+            vector_copy(bit, {"dp": partner(bit)}).start()
+
+        def end_across(bit):
+            vector_copy(bit, {"dp": partner(bit)}).wait()
+            vectors[...] += vectors_in[bit]
+
+        moves = [
+            (functools.partial(start_inward, hop), functools.partial(end_inward, hop))
+            for hop in range(half)
+        ]
+        moves += [
+            (functools.partial(start_outward, hop), functools.partial(end_outward, hop))
+            for hop in reversed(range(half - 1))
+        ]
+        moves += [
+            (functools.partial(start_across, bit), functools.partial(end_across, bit))
+            for bit in range(bits)
+        ]
+
+        def step(i):
+            if i > 0:
+                moves[i - 1][1]()
+            if i < len(moves):
+                moves[i][0]()
+
+        return [functools.partial(step, i) for i in range(len(moves) + 1)]
 
 
     first_lanes = lax.broadcasted_iota(jnp.int32, (CHUNK, LANES), 1)
@@ -674,6 +748,14 @@
             def _():
                 load_qkv.wait()
 
+            spot = lax.broadcasted_iota(jnp.int32, (CHUNK, LANES), 0) + c * CHUNK
+            begin = jnp.zeros((CHUNK, LANES), jnp.int32)
+            end = jnp.int32(0)
+            for i in range(lengths.shape[1]):
+                end = end + lengths[0, i]
+                begin = jnp.where(spot >= end, end, begin)
+            cosine[rows], sine[rows] = rotary_tables(spot, begin)
+
             for h in range(local_heads):
                 cols = slice(h * HEAD_DIM, (h + 1) * HEAD_DIM)
                 base = h * 3 * HEAD_DIM
@@ -688,7 +770,7 @@
 
             place = lax.broadcasted_iota(jnp.int32, (CHUNK, count), 1)
             here = lax.broadcasted_iota(jnp.int32, (CHUNK, count), 0) + c * CHUNK
-            allowed = (place >= start[rows, :1]) & (place <= here)
+            allowed = (place >= begin[:, :1]) & (place <= here)
             for h in range(local_heads):
                 cols = slice(h * HEAD_DIM, (h + 1) * HEAD_DIM)
                 scores = dot_cols(queries[:, cols], keys[:, cols]) * scale
@@ -834,7 +916,7 @@
     def fill(source, target, sem):
         return pltpu.make_async_copy(source, target, sem)
 
-    def spread_columns(number, left_source, first_slot, split):
+    def spread_columns(number, left_source, split):
         plan, _ = spreads[number]
         depth = left_source.shape[1]
 
@@ -861,9 +943,9 @@
 
             tiles_out(number, compute, tile, sems)
             if split:
-                service(first_slot)
+                next_slot()
             tiles_kept(number, compute, tile, landed, sems)
-            service(first_slot + split)
+            next_slot()
 
         pl.run_scoped(
             run,
@@ -875,18 +957,19 @@
             pltpu.SemaphoreType.DMA((3,)),
         )
 
-    def spread_rows(number, left_source, right_source, first_slot, split):
+    def spread_rows(number, left_source, right_source):
         plan, _ = spreads[number]
+        resident = right_source is joined_grad
 
         def run(left, right, tile, landed, sems):
             loads = [fill(left_source, left, sems.at[0])]
-            if right_source is not joined_grad:
+            if not resident:
                 loads.append(fill(right_source, right, sems.at[1]))
             for copy in loads:
                 copy.start()
             for copy in loads:
                 copy.wait()
-            use = joined_grad if right_source is joined_grad else right
+            use = joined_grad if resident else right
 
             def compute(where, target):
                 turned = left[:, span(where * plan.rows, plan.rows)].T
@@ -898,16 +981,14 @@
                     target[:, there] = dot(turned, use[:, there])
 
             tiles_out(number, compute, tile, sems)
-            if split:
-                service(first_slot)
+            next_slot()
             tiles_kept(number, compute, tile, landed, sems)
-            service(first_slot + split)
-
-        right_shape = (16, LANES) if right_source is joined_grad else (count, plan.cols)
+            next_slot()
+
         pl.run_scoped(
             run,
             pltpu.VMEM((count, width), BF16),
-            pltpu.VMEM(right_shape, BF16),
+            pltpu.VMEM((16, LANES) if resident else (count, plan.cols), BF16),
             pltpu.VMEM((2, plan.rows, plan.cols), F32),
             pltpu.VMEM((plan.rows, plan.cols), F32),
             pltpu.SemaphoreType.DMA((3,)),
@@ -915,10 +996,11 @@
 
     QKV, DENSE, UP, DOWN = range(4)
     slots = [2 * steps]
-
-    def take_slots(number):
-        slots[0] += number
-        return slots[0] - number
+    waiting = vector_steps()
+
+    def next_slot():
+        service(slots[0])
+        slots[0] += 1
 
     def with_weights(qkv, up, w_sems):
         load_qkv = pltpu.make_async_copy(qkv_weight, qkv, w_sems.at[0])
@@ -947,9 +1029,10 @@
             pltpu.SemaphoreType.DMA((5,)),
             pltpu.SemaphoreType.DMA((1,)),
         )
-        spread_columns(DOWN, hidden, take_slots(2), 1)
-        spread_columns(DENSE, attended, take_slots(1), 0)
-        first = take_slots(steps)
+        spread_columns(DOWN, hidden, True)
+        spread_rows(UP, mlp_entry, hidden_grad)
+        first = slots[0]
+        slots[0] += steps
         pl.run_scoped(
             lambda *scratch: backward(qkv, up, *scratch, first),
             pltpu.VMEM((2, CHUNK, inner_width), BF16),
@@ -966,18 +1049,27 @@
         pltpu.VMEM(up_weight.shape, BF16),
         pltpu.SemaphoreType.DMA((2,)),
     )
-    spread_rows(UP, mlp_entry, hidden_grad, take_slots(2), 1)
-    spread_rows(QKV, attn_entry, joined_grad, take_slots(2), 1)
-    for stage in range(1, bits - 1):
-        for number in (DOWN, DENSE, UP, QKV):
-            for side in range(2):
-                combine(number, stage, side)
-                if number != DENSE or side:
-                    service(take_slots(1))
-    for bit in range(bits):
-        sum_vectors_dp(bit)
-    service(take_slots(1))
-    sum_vectors_mp()
+
+    work = [
+        functools.partial(spread_columns, DENSE, attended, False),
+        functools.partial(spread_rows, QKV, attn_entry, joined_grad),
+    ]
+    for stage in range(1, bits):
+        for number in (DOWN, UP, DENSE, QKV):
+            for sides in ((0,), (1,)) if number != DENSE and stage < bits - 1 else ((0, 1),):
+
+                def task(number=number, stage=stage, sides=sides):
+                    for side in sides:
+                        combine(number, stage, side)
+                    next_slot()
+
+                work.append(task)
+    done = 0
+    for i, task in enumerate(work):
+        while done * len(work) < (i + 1) * len(waiting) and done < len(waiting):
+            waiting[done]()
+            done += 1
+        task()
 
     @pl.loop(slots[0], messages + half)
     def _(j):
@@ -1004,6 +1096,7 @@
         Spread(bits, owned, inner_width),
         Spread(bits, inner_width, owned),
     )
+    exchanges = bits + 2 * (mp_size // 2)
     vector_width = max(width, inner_width, qkv.shape[1])
     anywhere = pl.BlockSpec(memory_space=pl.ANY)
     vmem = pl.BlockSpec(memory_space=pltpu.VMEM)
@@ -1013,6 +1106,7 @@
         shape((count, width), BF16),
         shape((VECTORS, vector_width), F32),
         shape((2 * count, width), F32),
+        *(shape((plan.rows, plan.cols), F32) for plan in plans),
         shape((count, width), BF16),
         shape((count, width), BF16),
         shape((count, heads_width), BF16),
@@ -1030,8 +1124,10 @@
         pltpu.VMEM((2, ROWS, width), BF16),
         pltpu.VMEM((2, ROWS, width), BF16),
         pltpu.VMEM((VECTORS, vector_width), F32),
-        pltpu.VMEM((bits + 3, VECTORS, vector_width), F32),
+        pltpu.VMEM((exchanges, VECTORS, vector_width), F32),
         pltpu.VMEM((count, qkv.shape[1]), BF16),
+        pltpu.VMEM((count, LANES), F32),
+        pltpu.VMEM((count, LANES), F32),
         dma((messages,)),
         dma((messages,)),
         dma((messages,)),
@@ -1039,15 +1135,15 @@
         dma((2,)),
         dma((2, 2)),
         dma((2,)),
-        dma((bits + 3,)),
-        dma((bits + 3,)),
+        dma((exchanges,)),
+        dma((exchanges,)),
     ]
     for plan in plans:
         scratch += [dma((plan.sems,)), dma((plan.sems,))]
     results = pl.pallas_call(
         functools.partial(layer_kernel, mp_size, plans),
         out_shape=tuple(out_shape),
-        in_specs=[anywhere] * 6 + [vmem] * 10,
+        in_specs=[anywhere] * 6 + [vmem] * 7 + [pl.BlockSpec(memory_space=pltpu.SMEM)],
         out_specs=(anywhere,) * len(out_shape),
         scratch_shapes=scratch,
         compiler_params=pltpu.CompilerParams(
@@ -1059,13 +1155,48 @@
             transcendentals=0,
         ),
     )(*operands)
-    layer_output, input_grad, vectors = results[:3]
-    spread = list(results[9:])
-    grads = []
-    for plan in plans:
-        buffers, spread = spread[: 1 + bits], spread[1 + bits :]
-        grads.append(buffers[0][0] + buffers[bits][0])
-    return layer_output, input_grad, vectors, grads
+    return results[:3], results[4 : 4 + len(plans)]
+
+
+def hand_out(dp_size, totals, *refs):
+    refs = list(refs)
+    vectors = refs.pop(0)
+    number = (len(refs) - 1 - len(totals)) // 3
+    sources, refs = refs[:number], refs[number:]
+    targets, refs = refs[:number], refs[number:]
+    pieces, refs = refs[: len(totals)], refs[len(totals) :]
+    held, sems = refs[:number], refs[number]
+    loads = [pltpu.make_async_copy(a, b, sems.at[0, i]) for i, (a, b) in enumerate(zip(sources, held))]
+    stores = [pltpu.make_async_copy(a, b, sems.at[1, i]) for i, (a, b) in enumerate(zip(held, targets))]
+    for copy in loads:
+        copy.start()
+    width = vectors.shape[1]
+    for row, (total, piece) in enumerate(zip(totals, pieces)):
+        size = total // dp_size
+        shift = lax.rem(width - lax.axis_index("dp") * size, width)
+        piece[...] = pltpu.roll(vectors[...], shift, 1)[row : row + 1, :size]
+    for load, store in zip(loads, stores):
+        load.wait()
+        store.start()
+    for copy in stores:
+        copy.wait()
+
+
+def hand_out_call(dp_size, totals, vectors, arrays):
+    anywhere = pl.BlockSpec(memory_space=pl.ANY)
+    vmem = pl.BlockSpec(memory_space=pltpu.VMEM)
+    shape = jax.ShapeDtypeStruct
+    results = pl.pallas_call(
+        functools.partial(hand_out, dp_size, totals),
+        out_shape=[shape(array.shape, array.dtype) for array in arrays]
+        + [shape((1, total // dp_size), F32) for total in totals],
+        in_specs=[vmem] + [anywhere] * len(arrays),
+        out_specs=[anywhere] * len(arrays) + [vmem] * len(totals),
+        scratch_shapes=[pltpu.VMEM(array.shape, array.dtype) for array in arrays]
+        + [pltpu.SemaphoreType.DMA((2, len(arrays)))],
+        compiler_params=pltpu.CompilerParams(vmem_limit_bytes=62 * 1024 * 1024),
+    )(vectors, *arrays)
+    return results[: len(arrays)], [piece[0] for piece in results[len(arrays) :]]
 
 
 def per_device(
@@ -1086,11 +1217,8 @@
     out_bias,
     cotangent,
 ):
-    count, width = tokens.shape
-    start = layout(lengths[0], count)
-    cosine, sine = rotary_tables(start, count)
-    start = jnp.broadcast_to(start[:, None], (count, LANES))
-    layer_output, input_grad, vectors, grads = layer_call(
+    width = tokens.shape[1]
+    (layer_output, input_grad, vectors), grads = layer_call(
         mp_size,
         dp_size,
         (
@@ -1107,31 +1235,27 @@
             qkv_bias[None],
             up_bias[None],
             out_bias[None],
-            cosine,
-            sine,
-            start,
+            lengths,
         ),
     )
-    qkv_grad, dense_grad, up_grad, down_grad = grads
-    me = lax.axis_index("dp")
-
-    def owned(row, total):
-        return lax.dynamic_slice_in_dim(vectors[row], me * (total // dp_size), total // dp_size)
-
+    totals = (width,) * 5 + (up_weight.shape[1], qkv_weight.shape[1])
+    arrays, pieces = hand_out_call(dp_size, totals, vectors, (layer_output, input_grad, *grads))
+    layer_output, input_grad, qkv_grad, dense_grad, up_grad, down_grad = arrays
+    attn_gain_grad, attn_shift_grad, mlp_gain_grad, mlp_shift_grad = pieces[:4]
     return (
         layer_output,
         input_grad,
-        owned(ATTN_GAIN, width),
-        owned(ATTN_SHIFT, width),
-        owned(MLP_GAIN, width),
-        owned(MLP_SHIFT, width),
+        attn_gain_grad,
+        attn_shift_grad,
+        mlp_gain_grad,
+        mlp_shift_grad,
         qkv_grad,
-        owned(QKV_BIAS, qkv_weight.shape[1]),
+        pieces[QKV_BIAS],
         dense_grad,
         up_grad,
-        owned(UP_BIAS, up_weight.shape[1]),
+        pieces[UP_BIAS],
         down_grad,
-        owned(OUT_BIAS, width),
+        pieces[OUT_BIAS],
     )
 
 

time: 523 us -> 470 us (0.90)
  Pallas kernels: 489 us -> 467 us
  other arithmetic: 16.5 us -> 0 us
  local copies, waits for them, and re-layouts: 14.5 us -> 1.29 us
    pallas_call x1, Pallas kernels: 489 us -> 455 us  [layer_call(): pl.pallas_call(functools.partial(layer_kernel, mp_size, plans), out_shape...]
    add x4 -> x0, other arithmetic: 11.8 us -> none  [layer_call(): grads.append(buffers[0][0] + buffers[bits][0])]
    pallas_call x0 -> x1, Pallas kernels: none -> 11.7 us  [hand_out_call(): pl.pallas_call(functools.partial(hand_out, dp_size, totals), out_shape=[s...]
    unnamed x10 -> x0, local copies, waits for them, and re-layouts: 6.97 us -> none
where the time goes in v4:
time: 470 us; the launch traced here: 469 us
  Pallas kernels  467 us (99%)
    pallas_call x1, Pallas kernels, layer_call(): pl.pallas_call(functools.partial(layer_kernel, mp_size, plans), out_shape...  455 us
    pallas_call x1, Pallas kernels, hand_out_call(): pl.pallas_call(functools.partial(hand_out, dp_size, totals), out_shape=[s...  11.7 us

profile of v4, /device:TPU:0, one launch (start us, length us, event | category | flops | bytes accessed | tf_op | source)
XLA Modules:
  0.0 468.7 jit_solution(1581318201000772339)
XLA Ops:
  0.6 1.3 broadcast_in_dim.25.refs_10_
  1.9 454.9 %shard_map.237 = (bf16[1024,2048]{1,0:T(8,128)(2,1)}, bf16[1024,2048]{1,0:T(8,128)(2,1)}, f32[8,2048]{1,0:T(8,128)}, f32[2048,2048]{1,0:T(8,128)}, f32[256,1536]...) custom-call(bf16[1024,2048]{1,0:T(8,128)(2,1)} %refs_0_.1, ...), custom_call_target="tpu_custom_call" | custom-call | flops 77309411328 | bytes 314572800 | tf_op jit(solution)/shard_map/pallas_call | solution.py:1143
  456.8 11.7 %shard_map.238 = (bf16[1024,2048]{1,0:T(8,128)(2,1)}, bf16[1024,2048]{1,0:T(8,128)(2,1)}, f32[256,1536]{1,0:T(8,128)}, f32[512,256]{1,0:T(8,128)}, f32[256,2048]...) custom-call(f32[8,2048]{1,0:T(8,128)} %get-tuple-element.33.refs_0_,, ...), custom_call_target="tpu_custom_call" | custom-call | tf_op jit(solution)/shard_map/pallas_call | solution.py:1189

commit v5 on v4

--- a/solution.py
+++ b/solution.py
@@ -14,9 +14,12 @@
 LANES = 128
 
 MESH = pl.DeviceIdType.MESH
-ROWS = 64
-SLOTS = 6
-AHEAD = 2
+ROWS = 32
+SLOTS = 10
+AHEAD = 5
+AHEAD_ODD = 5
+PENDING = 3
+LAG = 1
 CHUNK = 256
 BLOCK = 32
 
@@ -137,7 +140,7 @@
     grads_out = take(len(plans))
     attn_entry, mlp_entry, attended, hidden, hidden_grad = take(5)
     spreads = [(plan, take(1 + plan.bits)) for plan in plans]
-    from_outer, from_inner, sums, token_rows, cot_rows, out_rows = take(6)
+    from_outer, held, token_rows, cot_rows, out_rows = take(5)
     vectors, vectors_in, joined_grad, cosine, sine = take(5)
     send_in, send_out, recv_outer, recv_inner, part_sems, row_sems, out_sems = take(7)
     vec_send, vec_recv = take(2)
@@ -160,10 +163,12 @@
     level = index * (1 - upper) + (mp_size - 1 - index) * upper
     inner = index + 1 - 2 * upper
     outer = index - 1 + 2 * upper
-    lag = half - level
-    ahead = min(AHEAD, SLOTS - 1 - half)
+    lag = half - level + LAG
+    ahead = min(AHEAD, SLOTS - 1 - LAG - half)
     is_middle = level == half - 1
+    total_place = (1 - level // (half - 1)) * SLOTS if half > 1 else 0
     device = lax.axis_index("dp")
+    ahead = ahead + (device % 2) * (min(AHEAD_ODD, SLOTS - 1 - LAG - half) - ahead)
 
     def partner(bit):
         return device + (1 - 2 * ((device // (1 << bit)) % 2)) * (1 << bit)
@@ -174,27 +179,37 @@
             total = total + ((device // (1 << bit) + mask // (1 << bit)) % 2) * (1 << bit)
         return total
 
-    barrier = pltpu.get_barrier_semaphore()
-    pl.semaphore_signal(barrier, inc=1, device_id={"mp": inner}, device_id_type=MESH)
-    for bit in range(bits):
-        pl.semaphore_signal(barrier, inc=1, device_id={"dp": partner(bit)}, device_id_type=MESH)
-    if half > 1:
-
-        @pl.when(level > 0)
-        def _():
-            pl.semaphore_signal(barrier, inc=1, device_id={"mp": outer}, device_id_type=MESH)
-            pl.semaphore_wait(barrier, 2 + bits)
-
-        @pl.when(level == 0)
-        def _():
+    def meet():
+        barrier = pltpu.get_barrier_semaphore()
+        pl.semaphore_signal(barrier, inc=1, device_id={"mp": inner}, device_id_type=MESH)
+        for bit in range(bits):
+            pl.semaphore_signal(barrier, inc=1, device_id={"dp": partner(bit)}, device_id_type=MESH)
+        if half > 1:
+
+            @pl.when(level > 0)
+            def _():
+                pl.semaphore_signal(barrier, inc=1, device_id={"mp": outer}, device_id_type=MESH)
+                pl.semaphore_wait(barrier, 2 + bits)
+
+            @pl.when(level == 0)
+            def _():
+                pl.semaphore_wait(barrier, 1 + bits)
+
+        else:
             pl.semaphore_wait(barrier, 1 + bits)
-
-    else:
-        pl.semaphore_wait(barrier, 1 + bits)
 
 
     def slot(ref, k):
         return ref.at[lax.rem(k, SLOTS)]
+
+    def sums(k):
+        return held.at[lax.rem(k, SLOTS)]
+
+    def from_inner(k):
+        return held.at[lax.rem(k, SLOTS) + SLOTS]
+
+    def totals(k):
+        return held.at[lax.rem(k, SLOTS) + total_place]
 
     def message(ref, k):
         return ref.at[span(k * ROWS, ROWS)]
@@ -202,17 +217,17 @@
     def to_inner(k, source, landing, sem):
         return pltpu.make_async_remote_copy(
             src_ref=source,
-            dst_ref=slot(landing, k),
+            dst_ref=landing,
             send_sem=send_in.at[k],
             recv_sem=sem.at[k],
             device_id={"mp": inner},
             device_id_type=MESH,
         )
 
-    def to_outer(k, source):
+    def to_outer(k):
         return pltpu.make_async_remote_copy(
-            src_ref=slot(source, k),
-            dst_ref=slot(from_inner, k),
+            src_ref=totals(k),
+            dst_ref=from_inner(k),
             send_sem=send_out.at[k],
             recv_sem=recv_inner.at[k],
             device_id={"mp": outer},
@@ -220,7 +235,7 @@
         )
 
     def load_part(k):
-        return pltpu.make_async_copy(message(parts, k), slot(sums, k), part_sems.at[lax.rem(k, 2)])
+        return pltpu.make_async_copy(message(parts, k), sums(k), part_sems.at[lax.rem(k, 2)])
 
     def load_rows(k):
         row, place = lax.rem(k, branch_messages), lax.rem(k, 2)
@@ -244,11 +259,13 @@
 
             @pl.when((level == 0) & (k < messages))
             def _():
-                to_inner(k, message(parts, k), from_outer, recv_outer).start()
+                to_inner(k, message(parts, k), slot(from_outer, k), recv_outer).start()
 
     def begin_messages():
-        for k in range(ahead):
+        @pl.loop(0, ahead)
+        def _(k):
             send_ahead(k)
+
         for copy in load_rows(0):
             copy.start()
         if half > 1:
@@ -269,23 +286,24 @@
             def _():
                 load_part(j + 1).start()
 
-            mine = slot(sums, j)
+            mine = sums(j)
             if half > 1:
-                to_inner(j, mine, from_outer, recv_outer).wait_recv()
+                to_inner(j, mine, slot(from_outer, j), recv_outer).wait_recv()
                 mine[...] += slot(from_outer, j)[...]
 
             @pl.when(is_middle)
             def _():
-                to_inner(j, mine, from_inner, recv_inner).start()
+                to_inner(j, mine, from_inner(j), recv_inner).start()
 
             if half > 2:
 
                 @pl.when(level < half - 1)
                 def _():
-                    to_inner(j, mine, from_outer, recv_outer).start()
-
-    def finish(k, source):
+                    to_inner(j, mine, slot(from_outer, j), recv_outer).start()
+
+    def finish(k):
         place = lax.rem(k, 2)
+        source = totals(k)
 
         @pl.when(k < branch_messages)
         def _():
@@ -315,32 +333,21 @@
     def pass_outward(k):
         @pl.when((k >= 0) & (k < messages))
         def _():
-            landed = slot(from_inner, k)
-            total = slot(sums, k)
-            to_outer(k, sums).wait_recv()
-            to_inner(k, total, from_inner, recv_inner).wait_send()
+            to_inner(k, sums(k), from_inner(k), recv_inner).wait()
 
             @pl.when(is_middle)
             def _():
-                total[...] += landed[...]
+                sums(k)[...] += from_inner(k)[...]
 
             if half > 1:
 
                 @pl.when(level > 0)
                 def _():
-                    @pl.when(k >= 1)
+                    @pl.when(k >= PENDING)
                     def _():
-                        to_outer(k - 1, sums).wait_send()
-
-                    @pl.when(is_middle)
-                    def _():
-                        to_outer(k, sums).start()
-
-                    if half > 2:
-
-                        @pl.when(level < half - 1)
-                        def _():
-                            to_outer(k, from_inner).start()
+                        to_outer(k - PENDING).wait_send()
+
+                    to_outer(k).start()
 
             @pl.when(k + 1 < messages)
             def _():
@@ -354,15 +361,7 @@
             def _():
                 store_rows(k - 2, layer_out).wait()
 
-            @pl.when(is_middle)
-            def _():
-                finish(k, total)
-
-            if half > 1:
-
-                @pl.when(level < half - 1)
-                def _():
-                    finish(k, landed)
+            finish(k)
 
             @pl.when(k < branch_messages)
             def _():
@@ -389,7 +388,8 @@
 
             @pl.when(level > 0)
             def _():
-                to_outer(messages - 1, sums).wait_send()
+                for k in range(messages - PENDING, messages):
+                    to_outer(k).wait_send()
 
         for k in (messages - 2, messages - 1):
             store_rows(k, input_grad).wait()
@@ -430,14 +430,30 @@
                 )
         return copies
 
-    def tiles_out(number, compute, tile, sems):
+    def tiles_of(number, compute, sent, kept, landed, sems, first, each):
         plan, buffers = spreads[number]
         half_tiles = plan.tiles // 2
+        every = max(1, half_tiles // 4)
 
         def copy(i):
-            return spread_copy(
-                number, 0, 0, tile.at[lax.rem(i, 2)], buffers[1].at[i], i, 0
+            return spread_copy(number, 0, 0, sent.at[lax.rem(i, 2)], buffers[1].at[i], i, 0)
+
+        def load(i):
+            return pltpu.make_async_copy(buffers[1].at[i], landed, sems.at[0])
+
+        def store(i):
+            return pltpu.make_async_copy(
+                kept.at[lax.rem(i, 2)], buffers[0].at[i], sems.at[1 + lax.rem(i, 2)]
             )
+
+        def begin_add(i):
+            copy(i).wait_recv()
+            load(i).start()
+
+        def end_add(i):
+            load(i).wait()
+            kept.at[lax.rem(i, 2)][...] += landed[...]
+            store(i).start()
 
         @pl.loop(0, half_tiles)
         def _(i):
@@ -445,45 +461,43 @@
             def _():
                 copy(i - 2).wait_send()
 
-            compute(owner(2 * i + 1), tile.at[lax.rem(i, 2)])
+            compute(owner(2 * i + 1), sent.at[lax.rem(i, 2)])
             copy(i).start()
 
+            @pl.when(i >= 1)
+            def _():
+                begin_add(i - 1)
+
+            if each == 2:
+
+                @pl.when(lax.rem(i, every) == every - 1)
+                def _():
+                    service(first + 2 * (i // every))
+
+            @pl.when(i >= 2)
+            def _():
+                store(i - 2).wait()
+
+            compute(owner(2 * i), kept.at[lax.rem(i, 2)])
+
+            @pl.when(i >= 1)
+            def _():
+                end_add(i - 1)
+
+            if each >= 1:
+
+                @pl.when(lax.rem(i, every) == every - 1)
+                def _():
+                    service(first + each * (i // every) + each - 1)
+
+        begin_add(half_tiles - 1)
+        end_add(half_tiles - 1)
         for i in (half_tiles - 2, half_tiles - 1):
             copy(i).wait_send()
-
-    def tiles_kept(number, compute, tile, landed, sems):
-        plan, buffers = spreads[number]
-        half_tiles = plan.tiles // 2
-
-        def load(i):
-            return pltpu.make_async_copy(buffers[1].at[i], landed, sems.at[0])
-
-        def store(i):
-            return pltpu.make_async_copy(
-                tile.at[lax.rem(i, 2)], buffers[0].at[i], sems.at[1 + lax.rem(i, 2)]
-            )
-
-        @pl.loop(0, half_tiles)
-        def _(i):
-            spread_copy(
-                number, 0, 0, tile.at[0], buffers[1].at[i], i, 0
-            ).wait_recv()
-            load(i).start()
-
-            @pl.when(i >= 2)
-            def _():
-                store(i - 2).wait()
-
-            compute(owner(2 * i), tile.at[lax.rem(i, 2)])
-            load(i).wait()
-            tile.at[lax.rem(i, 2)][...] += landed[...]
-            store(i).start()
-
-        for i in (half_tiles - 2, half_tiles - 1):
             store(i).wait()
         for side in range(2):
-            for copy in stage_copies(number, 1, side):
-                copy.start()
+            for copies in stage_copies(number, 1, side):
+                copies.start()
 
     def combine(number, stage, side):
         plan, buffers = spreads[number]
@@ -491,15 +505,17 @@
         last = stage == bits - 1
         rows = plan.rows // 4
 
+        masks = plan.masks(side, stage + 1)
+
         def run(mine, other, sems):
             for copy in stage_copies(number, stage, side):
                 copy.wait_recv()
             loads, stores = [], []
-            for mask in plan.masks(side, stage + 1):
+            for mask in masks:
                 place = plan.place(mask, side, stage)
                 for piece in range(2):
                     there = pl.ds(side * (plan.rows // 2) + piece * rows, rows)
-                    at = len(loads) % 2
+                    at = len(loads)
                     kept = keep.at[mask // 2, there]
                     loads.append(
                         [
@@ -511,27 +527,27 @@
                     )
                     target = grads_out[number].at[there] if last else kept
                     stores.append(pltpu.make_async_copy(mine.at[at], target, sems.at[2, at]))
-            for copy in loads[0]:
-                copy.start()
+            for load in loads:
+                for copy in load:
+                    copy.start()
             for i, (load, store) in enumerate(zip(loads, stores)):
-                if i + 1 < len(loads):
-                    if i >= 1:
-                        stores[i - 1].wait()
-                    for copy in loads[i + 1]:
-                        copy.start()
                 for copy in load:
                     copy.wait()
-                mine[i % 2] += other[i % 2]
+                mine[i] += other[i]
                 store.start()
-            for store in stores[-2:]:
+            for store in stores:
                 store.wait()
             if not last:
                 for copy in stage_copies(number, stage + 1, side):
                     copy.start()
 
-        shape = (2, rows, plan.cols)
+        pieces = 2 * len(masks)
+        shape = (pieces, rows, plan.cols)
         pl.run_scoped(
-            run, pltpu.VMEM(shape, F32), pltpu.VMEM(shape, F32), pltpu.SemaphoreType.DMA((3, 2))
+            run,
+            pltpu.VMEM(shape, F32),
+            pltpu.VMEM(shape, F32),
+            pltpu.SemaphoreType.DMA((3, pieces)),
         )
 
     def end_spread(number):
@@ -667,6 +683,7 @@
         mlp_chunk,
         hidden_chunk,
         hidden_grad_chunk,
+        slope,
         part,
         probs,
         queries,
@@ -712,14 +729,26 @@
         load_tokens(0).start()
         load_qkv.start()
         load_up.start()
+        load_down.start()
         load_dense.start()
         load_cot(0).start()
-        load_down.start()
+        meet()
         keys[...] = jnp.zeros_like(keys)
         values[...] = jnp.zeros_like(values)
         key_grad[...] = jnp.zeros_like(key_grad)
         value_grad[...] = jnp.zeros_like(value_grad)
         vectors[...] = jnp.zeros_like(vectors)
+
+        def by_extent(c, function):
+            low = 0
+            while low < steps:
+                high = min(steps, max(2 * low, 1))
+
+                @pl.when((c >= low) & (c < high))
+                def _():
+                    function(high * CHUNK)
+
+                low = high
 
         @pl.loop(0, steps)
         def _(c):
@@ -768,37 +797,42 @@
                 keys[rows, cols] = turn(joined(1), rows, 1.0).astype(BF16)
                 values[rows, cols] = joined(2).astype(BF16)
 
-            place = lax.broadcasted_iota(jnp.int32, (CHUNK, count), 1)
-            here = lax.broadcasted_iota(jnp.int32, (CHUNK, count), 0) + c * CHUNK
-            allowed = (place >= begin[:, :1]) & (place <= here)
-            for h in range(local_heads):
-                cols = slice(h * HEAD_DIM, (h + 1) * HEAD_DIM)
-                scores = dot_cols(queries[:, cols], keys[:, cols]) * scale
-                scores = jnp.where(allowed, scores, -1e30)
-                expo = jnp.exp(scores - jnp.max(scores, axis=-1, keepdims=True))
-                prob = expo * (1.0 / jnp.sum(expo, axis=-1, keepdims=True))
-                probs[h] = prob
-                attended_chunk[:, cols] = dot(prob.astype(BF16), values[:, cols]).astype(BF16)
+            def attend(extent):
+                place = lax.broadcasted_iota(jnp.int32, (CHUNK, extent), 1)
+                here = lax.broadcasted_iota(jnp.int32, (CHUNK, extent), 0) + c * CHUNK
+                allowed = (place >= begin[:, :1]) & (place <= here)
+                for h in range(local_heads):
+                    cols = slice(h * HEAD_DIM, (h + 1) * HEAD_DIM)
+                    scores = dot_cols(queries[:, cols], keys[:extent, cols]) * scale
+                    scores = jnp.where(allowed, scores, -1e30)
+                    expo = jnp.exp(scores - jnp.max(scores, axis=-1, keepdims=True))
+                    prob = expo * (1.0 / jnp.sum(expo, axis=-1, keepdims=True))
+                    probs[h, :, :extent] = prob
+                    attended_chunk[:, cols] = dot(prob.astype(BF16), values[:extent, cols]).astype(
+                        BF16
+                    )
+
+            by_extent(c, attend)
+
+            @pl.when(c > 0)
+            def _():
+                service(c * 4 - 2)
 
             @pl.when(c == 0)
             def _():
                 load_up.wait()
-                load_down.wait()
-
-            load_cot(c).wait()
 
             @pl.loop(0, inner_width // tile)
             def _(t):
                 cols = span(t * tile, tile)
                 pre = dot(mlp_chunk[...], up[:, cols]) + up_bias[:, cols]
-                value, slope = gelu_parts(pre)
+                value, derivative = gelu_parts(pre)
                 hidden_chunk[:, cols] = value.astype(BF16)
-                grad = (slope * dot_cols(cot[...], down[cols, :])).astype(BF16)
-                hidden_grad_chunk[:, cols] = grad
-                vectors[UP_BIAS : UP_BIAS + 1, cols] += column_sum(grad.astype(F32))
+                slope[:, cols] = derivative
 
             @pl.when(c == 0)
             def _():
+                load_down.wait()
                 load_dense.wait()
 
             @pl.loop(0, width // wide)
@@ -814,33 +848,49 @@
             def _():
                 begin_messages()
 
+            @pl.when(c > 0)
+            def _():
+                service(c * 4 - 1)
+
+            load_cot(c).wait()
+
+            @pl.loop(0, inner_width // tile)
+            def _(t):
+                cols = span(t * tile, tile)
+                grad = (slope[:, cols] * dot_cols(cot[...], down[cols, :])).astype(BF16)
+                hidden_grad_chunk[:, cols] = grad
+                vectors[UP_BIAS : UP_BIAS + 1, cols] += column_sum(grad.astype(F32))
+
             for copy in chunk_stores(c):
                 copy.start()
 
-            service(2 * c)
-
+            service(c * 4)
             attended_grad[...] = dot_cols(cot[...], dense[...]).astype(BF16)
-            for h in range(local_heads):
-                cols = slice(h * HEAD_DIM, (h + 1) * HEAD_DIM)
-                base = h * 3 * HEAD_DIM
-                grad = attended_grad[:, cols]
-                prob = probs[h]
-                prob_grad = dot_cols(grad, values[:, cols])
-                along = jnp.sum(prob * prob_grad, axis=-1, keepdims=True)
-                score_grad = (prob * (prob_grad - along)).astype(BF16)
-                query_grad = dot(score_grad, keys[:, cols]) * scale
-                joined_grad[rows, base : base + HEAD_DIM] = turn(query_grad, rows, -1.0).astype(
-                    BF16
-                )
-                key_grad[:, cols] += dot_rows(score_grad, queries[:, cols]) * scale
-                value_grad[:, cols] += dot_rows(prob.astype(BF16), grad)
+
+            def attend_back(extent):
+                for h in range(local_heads):
+                    cols = slice(h * HEAD_DIM, (h + 1) * HEAD_DIM)
+                    base = h * 3 * HEAD_DIM
+                    grad = attended_grad[:, cols]
+                    prob = probs[h, :, :extent]
+                    prob_grad = dot_cols(grad, values[:extent, cols])
+                    along = jnp.sum(prob * prob_grad, axis=-1, keepdims=True)
+                    score_grad = (prob * (prob_grad - along)).astype(BF16)
+                    query_grad = dot(score_grad, keys[:extent, cols]) * scale
+                    joined_grad[rows, base : base + HEAD_DIM] = turn(query_grad, rows, -1.0).astype(
+                        BF16
+                    )
+                    key_grad[:extent, cols] += dot_rows(score_grad, queries[:, cols]) * scale
+                    value_grad[:extent, cols] += dot_rows(prob.astype(BF16), grad)
+
+            by_extent(c, attend_back)
 
             @pl.loop(0, CHUNK // BLOCK)
             def _(b):
                 block = span(b * BLOCK, BLOCK)
                 vectors[OUT_BIAS : OUT_BIAS + 1, :width] += column_sum(cot[block].astype(F32))
 
-            service(2 * c + 1)
+            service(c * 4 + 1)
 
         for copy in chunk_stores(steps - 1):
             copy.wait()
@@ -910,17 +960,21 @@
                 ):
                     vectors[row : row + 1, cols] += column_sum(value)
 
+                @pl.when(t == width // wide // 2 - 1)
+                def _():
+                    service(first_slot + 2 * c)
+
             store_part(steps + c, part, part_sem.at[0])
-            service(first_slot + c)
+            service(first_slot + 2 * c + 1)
 
     def fill(source, target, sem):
         return pltpu.make_async_copy(source, target, sem)
 
-    def spread_columns(number, left_source, split):
+    def spread_columns(number, left_source, each):
         plan, _ = spreads[number]
         depth = left_source.shape[1]
 
-        def run(left, turned, right, tile, landed, sems):
+        def run(left, turned, right, sent, kept, landed, sems):
             loads = [fill(left_source, left, sems.at[0]), fill(cotangent, right, sems.at[1])]
             for copy in loads:
                 copy.start()
@@ -941,11 +995,9 @@
                     there = span(b * block, block)
                     target[there, :] = dot(turned[there, :], right_cols)
 
-            tiles_out(number, compute, tile, sems)
-            if split:
+            tiles_of(number, compute, sent, kept, landed, sems, take_slots(4 * each), each)
+            if not each:
                 next_slot()
-            tiles_kept(number, compute, tile, landed, sems)
-            next_slot()
 
         pl.run_scoped(
             run,
@@ -953,15 +1005,16 @@
             pltpu.VMEM((depth, count), BF16),
             pltpu.VMEM((count, width), BF16),
             pltpu.VMEM((2, plan.rows, plan.cols), F32),
+            pltpu.VMEM((2, plan.rows, plan.cols), F32),
             pltpu.VMEM((plan.rows, plan.cols), F32),
             pltpu.SemaphoreType.DMA((3,)),
         )
 
-    def spread_rows(number, left_source, right_source):
+    def spread_rows(number, left_source, right_source, each):
         plan, _ = spreads[number]
         resident = right_source is joined_grad
 
-        def run(left, right, tile, landed, sems):
+        def run(left, right, sent, kept, landed, sems):
             loads = [fill(left_source, left, sems.at[0])]
             if not resident:
                 loads.append(fill(right_source, right, sems.at[1]))
@@ -980,27 +1033,28 @@
                     there = span(b * block, block)
                     target[:, there] = dot(turned, use[:, there])
 
-            tiles_out(number, compute, tile, sems)
-            next_slot()
-            tiles_kept(number, compute, tile, landed, sems)
-            next_slot()
+            tiles_of(number, compute, sent, kept, landed, sems, take_slots(4 * each), each)
 
         pl.run_scoped(
             run,
             pltpu.VMEM((count, width), BF16),
             pltpu.VMEM((16, LANES) if resident else (count, plan.cols), BF16),
             pltpu.VMEM((2, plan.rows, plan.cols), F32),
+            pltpu.VMEM((2, plan.rows, plan.cols), F32),
             pltpu.VMEM((plan.rows, plan.cols), F32),
             pltpu.SemaphoreType.DMA((3,)),
         )
 
     QKV, DENSE, UP, DOWN = range(4)
-    slots = [2 * steps]
+    slots = [4 * steps - 2]
     waiting = vector_steps()
 
+    def take_slots(number):
+        slots[0] += number
+        return slots[0] - number
+
     def next_slot():
-        service(slots[0])
-        slots[0] += 1
+        service(take_slots(1))
 
     def with_weights(qkv, up, w_sems):
         load_qkv = pltpu.make_async_copy(qkv_weight, qkv, w_sems.at[0])
@@ -1019,6 +1073,7 @@
             pltpu.VMEM((CHUNK, width), BF16),
             pltpu.VMEM((CHUNK, inner_width), BF16),
             pltpu.VMEM((CHUNK, inner_width), BF16),
+            pltpu.VMEM((CHUNK, inner_width), F32),
             pltpu.VMEM((CHUNK, width), F32),
             pltpu.VMEM((local_heads, CHUNK, count), F32),
             pltpu.VMEM((CHUNK, heads_width), BF16),
@@ -1029,10 +1084,9 @@
             pltpu.SemaphoreType.DMA((5,)),
             pltpu.SemaphoreType.DMA((1,)),
         )
-        spread_columns(DOWN, hidden, True)
-        spread_rows(UP, mlp_entry, hidden_grad)
-        first = slots[0]
-        slots[0] += steps
+        spread_columns(DOWN, hidden, 2)
+        spread_rows(UP, mlp_entry, hidden_grad, 1)
+        first = take_slots(2 * steps)
         pl.run_scoped(
             lambda *scratch: backward(qkv, up, *scratch, first),
             pltpu.VMEM((2, CHUNK, inner_width), BF16),
@@ -1050,20 +1104,27 @@
         pltpu.SemaphoreType.DMA((2,)),
     )
 
+    def several(number):
+        first = take_slots(number)
+
+        @pl.loop(first, first + number)
+        def _(k):
+            service(k)
+
+    def combines(number, stage):
+        for side in range(2):
+            combine(number, stage, side)
+            next_slot()
+
     work = [
-        functools.partial(spread_columns, DENSE, attended, False),
-        functools.partial(spread_rows, QKV, attn_entry, joined_grad),
+        functools.partial(spread_columns, DENSE, attended, 0),
+        functools.partial(spread_rows, QKV, attn_entry, joined_grad, 2),
     ]
     for stage in range(1, bits):
-        for number in (DOWN, UP, DENSE, QKV):
-            for sides in ((0,), (1,)) if number != DENSE and stage < bits - 1 else ((0, 1),):
-
-                def task(number=number, stage=stage, sides=sides):
-                    for side in sides:
-                        combine(number, stage, side)
-                    next_slot()
-
-                work.append(task)
+        for number, pause in ((DOWN, 1), (UP, 2), (DENSE, 0), (QKV, 3)):
+            work.append(functools.partial(combines, number, stage))
+            if pause and (stage < bits - 1 or number in (DOWN, UP)):
+                work.append(functools.partial(several, pause))
     done = 0
     for i, task in enumerate(work):
         while done * len(work) < (i + 1) * len(waiting) and done < len(waiting):
@@ -1071,7 +1132,7 @@
             done += 1
         task()
 
-    @pl.loop(slots[0], messages + half)
+    @pl.loop(slots[0], messages + half + LAG)
     def _(j):
         service(j)
 
@@ -1118,8 +1179,7 @@
     dma = pltpu.SemaphoreType.DMA
     scratch = [
         pltpu.VMEM((SLOTS, ROWS, width), F32),
-        pltpu.VMEM((SLOTS, ROWS, width), F32),
-        pltpu.VMEM((SLOTS, ROWS, width), F32),
+        pltpu.VMEM((2 * SLOTS, ROWS, width), F32),
         pltpu.VMEM((2, ROWS, width), BF16),
         pltpu.VMEM((2, ROWS, width), BF16),
         pltpu.VMEM((2, ROWS, width), BF16),

time: 470 us -> 438 us (0.932)
  Pallas kernels: 467 us -> 435 us
    pallas_call x1, Pallas kernels: 455 us -> 423 us  [layer_call(): pl.pallas_call(functools.partial(layer_kernel, mp_size, plans), out_shape...]
where the time goes in v5:
time: 438 us; the launch traced here: 437 us
  Pallas kernels  435 us (99%)
    pallas_call x1, Pallas kernels, layer_call(): pl.pallas_call(functools.partial(layer_kernel, mp_size, plans), out_shape...  423 us
    pallas_call x1, Pallas kernels, hand_out_call(): pl.pallas_call(functools.partial(hand_out, dp_size, totals), out_shape=[s...  11.7 us

profile of v5, /device:TPU:0, one launch (start us, length us, event | category | flops | bytes accessed | tf_op | source)
XLA Modules:
  0.0 437.1 jit_solution(7308540221129850713)
XLA Ops:
  0.6 1.3 broadcast_in_dim.25.refs_10_
  1.9 423.2 %shard_map.237 = (bf16[1024,2048]{1,0:T(8,128)(2,1)}, bf16[1024,2048]{1,0:T(8,128)(2,1)}, f32[8,2048]{1,0:T(8,128)}, f32[2048,2048]{1,0:T(8,128)}, f32[256,1536]...) custom-call(bf16[1024,2048]{1,0:T(8,128)(2,1)} %refs_0_.1, ...), custom_call_target="tpu_custom_call" | custom-call | flops 77309411328 | bytes 314572800 | tf_op jit(solution)/shard_map/pallas_call | solution.py:1203
  425.2 11.7 %shard_map.238 = (bf16[1024,2048]{1,0:T(8,128)(2,1)}, bf16[1024,2048]{1,0:T(8,128)(2,1)}, f32[256,1536]{1,0:T(8,128)}, f32[512,256]{1,0:T(8,128)}, f32[256,2048]...) custom-call(f32[8,2048]{1,0:T(8,128)} %get-tuple-element.33.refs_0_,, ...), custom_call_target="tpu_custom_call" | custom-call | tf_op jit(solution)/shard_map/pallas_call | solution.py:1249

commit v6 on v5

--- a/solution.py
+++ b/solution.py
@@ -1125,11 +1125,14 @@
             work.append(functools.partial(combines, number, stage))
             if pause and (stage < bits - 1 or number in (DOWN, UP)):
                 work.append(functools.partial(several, pause))
-    done = 0
-    for i, task in enumerate(work):
-        while done * len(work) < (i + 1) * len(waiting) and done < len(waiting):
-            waiting[done]()
-            done += 1
+    last = len(work) - 6
+    hops = len(waiting) - 1 - bits
+    places = [i * (last * 2 // 3) // hops for i in range(hops)]
+    places += [last + i * 6 // bits for i in range(bits)] + [len(work)]
+    for i, task in enumerate(work + [lambda: None]):
+        for place, step in zip(places, waiting):
+            if place == i:
+                step()
         task()
 
     @pl.loop(slots[0], messages + half + LAG)

time: 438 us -> 434 us (level)
  Pallas kernels: 435 us -> 430 us
    pallas_call x1, Pallas kernels: 423 us -> 419 us  [layer_call(): pl.pallas_call(functools.partial(layer_kernel, mp_size, plans), out_shape...]
where the time goes in v6:
time: 434 us; the launch traced here: 433 us
  Pallas kernels  430 us (99%)
    pallas_call x1, Pallas kernels, layer_call(): pl.pallas_call(functools.partial(layer_kernel, mp_size, plans), out_shape...  419 us
    pallas_call x1, Pallas kernels, hand_out_call(): pl.pallas_call(functools.partial(hand_out, dp_size, totals), out_shape=[s...  11.7 us

profile of v6, /device:TPU:0, one launch (start us, length us, event | category | flops | bytes accessed | tf_op | source)
XLA Modules:
  0.0 432.6 jit_solution(5478428316263803375)
XLA Ops:
  0.6 1.3 broadcast_in_dim.25.refs_10_
  1.9 418.7 %shard_map.237 = (bf16[1024,2048]{1,0:T(8,128)(2,1)}, bf16[1024,2048]{1,0:T(8,128)(2,1)}, f32[8,2048]{1,0:T(8,128)}, f32[2048,2048]{1,0:T(8,128)}, f32[256,1536]...) custom-call(bf16[1024,2048]{1,0:T(8,128)(2,1)} %refs_0_.1, ...), custom_call_target="tpu_custom_call" | custom-call | flops 77309411328 | bytes 314572800 | tf_op jit(solution)/shard_map/pallas_call | solution.py:1206
  420.7 11.7 %shard_map.238 = (bf16[1024,2048]{1,0:T(8,128)(2,1)}, bf16[1024,2048]{1,0:T(8,128)(2,1)}, f32[256,1536]{1,0:T(8,128)}, f32[512,256]{1,0:T(8,128)}, f32[256,2048]...) custom-call(f32[8,2048]{1,0:T(8,128)} %get-tuple-element.33.refs_0_,, ...), custom_call_target="tpu_custom_call" | custom-call | tf_op jit(solution)/shard_map/pallas_call | solution.py:1252

commit v7 on v6

--- a/solution.py
+++ b/solution.py
@@ -731,7 +731,6 @@
         load_up.start()
         load_down.start()
         load_dense.start()
-        load_cot(0).start()
         meet()
         keys[...] = jnp.zeros_like(keys)
         values[...] = jnp.zeros_like(values)
@@ -767,11 +766,6 @@
                 hat, _ = normalize(token_chunk[block].astype(F32))
                 attn_chunk[block] = (hat * attn_gain[...] + attn_shift[...]).astype(BF16)
                 mlp_chunk[block] = (hat * mlp_gain[...] + mlp_shift[...]).astype(BF16)
-
-            @pl.when(c + 1 < steps)
-            def _():
-                load_tokens(c + 1).start()
-                load_cot(c + 1).start()
 
             @pl.when(c == 0)
             def _():
@@ -834,6 +828,7 @@
             def _():
                 load_down.wait()
                 load_dense.wait()
+                load_cot(0).start()
 
             @pl.loop(0, width // wide)
             def _(t):
@@ -853,6 +848,11 @@
                 service(c * 4 - 1)
 
             load_cot(c).wait()
+
+            @pl.when(c + 1 < steps)
+            def _():
+                load_tokens(c + 1).start()
+                load_cot(c + 1).start()
 
             @pl.loop(0, inner_width // tile)
             def _(t):

time: 434 us -> 434 us (level)
  no operation moved by 1% of the time
where the time goes in v7:
time: 434 us; the launch traced here: 433 us
  Pallas kernels  430 us (99%)
    pallas_call x1, Pallas kernels, layer_call(): pl.pallas_call(functools.partial(layer_kernel, mp_size, plans), out_shape...  419 us
    pallas_call x1, Pallas kernels, hand_out_call(): pl.pallas_call(functools.partial(hand_out, dp_size, totals), out_shape=[s...  11.7 us

profile of v7, /device:TPU:0, one launch (start us, length us, event | category | flops | bytes accessed | tf_op | source)
XLA Modules:
  0.0 432.6 jit_solution(6727237412660931079)
XLA Ops:
  0.6 1.3 broadcast_in_dim.25.refs_10_
  1.9 418.7 %shard_map.237 = (bf16[1024,2048]{1,0:T(8,128)(2,1)}, bf16[1024,2048]{1,0:T(8,128)(2,1)}, f32[8,2048]{1,0:T(8,128)}, f32[2048,2048]{1,0:T(8,128)}, f32[256,1536]...) custom-call(bf16[1024,2048]{1,0:T(8,128)(2,1)} %refs_0_.1, ...), custom_call_target="tpu_custom_call" | custom-call | flops 77309411328 | bytes 314572800 | tf_op jit(solution)/shard_map/pallas_call | solution.py:1206
  420.7 11.7 %shard_map.238 = (bf16[1024,2048]{1,0:T(8,128)(2,1)}, bf16[1024,2048]{1,0:T(8,128)(2,1)}, f32[256,1536]{1,0:T(8,128)}, f32[512,256]{1,0:T(8,128)}, f32[256,2048]...) custom-call(f32[8,2048]{1,0:T(8,128)} %get-tuple-element.33.refs_0_,, ...), custom_call_target="tpu_custom_call" | custom-call | tf_op jit(solution)/shard_map/pallas_call | solution.py:1252
